TPU v7x, 512 devices: a whole 4x8x8 slice. The times are simulated.
512 devices in a mesh: crop: 4 (over y_hi), res: 128 (over y_lo, z, x, core).
Axes of the slice: x: 4, y: 8 (y_hi: 4, y_lo: 2; y = y_hi * 2 + y_lo), z: 8, core: 2. Of those that a mesh axis runs over, the one named last changes fastest.
Arguments:
- alignment_features: bfloat16 [512, 512, 256], P(('crop', 'res')), parts along dimension 0, may hold values from -6 to 6
- standardizer_scaling: float32 [256], replicated, may hold values from 0.1 to 1.9
- first_factor_matrix: bfloat16 [256, 32], replicated, may hold values from -0.375 to 0.375
- second_factor_matrix: bfloat16 [256, 32], replicated, may hold values from -0.375 to 0.375
- final_mixing_matrix: bfloat16 [1024, 128], replicated, may hold values from -2 to 2
- final_offset: float32 [128], replicated, may hold values from -4 to 4
Outputs:
- pair_update: bfloat16 [2048, 512, 128], P(('crop', 'res')), parts along dimension 0
There are 4 independent parts, one for each index of `crop`. A program takes and returns all parts, laid end to end along the dimension named above; an argument that names none is the same for every part. Nothing has to cross between parts.
All inputs are finite; a program needn't handle non-finite values.
Results may differ from a plain program's by a relative error of at most 0.0064.
Values may be sent and summed in bfloat16 or wider, within the bound.
No kernel may reach another device: no remote copies, remote signals or barrier semaphores. Data moves between devices by JAX's collectives and lax.ppermute only.
A program may use at most 64 MiB of HBM per device.

v0:
```python
import jax
import jax.numpy as jnp
from jax import lax
from jax.sharding import PartitionSpec as P


def standardize_features(values, gain):
    mean = jnp.mean(values, axis=-1, keepdims=True)
    centred = values - mean
    variance = jnp.mean(centred * centred, axis=-1, keepdims=True)
    return centred * lax.rsqrt(variance + 1e-05) * gain


def project_both(slice_indices, standardizer_scaling, first_factor_matrix, second_factor_matrix):
    leading_extent, tile_extent, feature_count = slice_indices.shape
    standardized_alignment = standardize_features(
        slice_indices.astype(jnp.float32), standardizer_scaling
    ).astype(jnp.bfloat16)
    unrolled_tensor = standardized_alignment.reshape(leading_extent * tile_extent, feature_count)
    first_factor = jnp.dot(
        unrolled_tensor, first_factor_matrix, preferred_element_type=jnp.float32
    ).astype(jnp.bfloat16)
    second_factor = jnp.dot(
        unrolled_tensor, second_factor_matrix, preferred_element_type=jnp.float32
    ).astype(jnp.bfloat16)
    factor = first_factor_matrix.shape[1]
    return (
        first_factor.reshape(leading_extent, tile_extent, factor),
        second_factor.reshape(leading_extent, tile_extent, factor),
    )


def block_width(columns):
    best = 1
    for candidate in range(1, min(columns, 160) + 1):
        if columns % candidate == 0:
            best = candidate
    return best


def body(
    alignment_features,
    standardizer_scaling,
    first_factor_matrix,
    second_factor_matrix,
    final_mixing_matrix,
    final_offset,
):
    gathered_slices = lax.all_to_all(
        alignment_features, "res", split_axis=1, concat_axis=0, tiled=True
    )
    first_factor, second_factor = project_both(
        gathered_slices, standardizer_scaling, first_factor_matrix, second_factor_matrix
    )
    seqs, own_rows, factor = first_factor.shape
    pair_width = final_mixing_matrix.shape[1]
    left_flat = first_factor.reshape(seqs, own_rows * factor)
    piece = lax.all_gather(second_factor, "res", axis=1, tiled=True)
    columns = piece.shape[1]
    tile_extent = block_width(columns)
    grouped = piece.reshape(seqs, columns // tile_extent, tile_extent, factor).transpose(1, 0, 2, 3)

    def one_block(right_block):
        right_flat = right_block.reshape(seqs, tile_extent * factor)
        tensor_products = (
            lax.dot_general(
                left_flat, right_flat, (((0,), (0,)), ((), ())), preferred_element_type=jnp.float32
            )
            / seqs
        )
        tensor_products = tensor_products.astype(jnp.bfloat16).reshape(
            own_rows, factor, tile_extent, factor
        )
        tensor_products = tensor_products.transpose(0, 2, 1, 3).reshape(
            own_rows * tile_extent, factor * factor
        )
        result = (
            jnp.dot(tensor_products, final_mixing_matrix, preferred_element_type=jnp.float32)
            + final_offset
        )
        return result.astype(jnp.bfloat16).reshape(own_rows, tile_extent, pair_width)

    stacked = lax.map(one_block, grouped)
    return stacked.transpose(1, 0, 2, 3).reshape(own_rows, columns, pair_width)


def solution(mesh):
    in_specs = (P(("crop", "res"), None, None), P(), P(), P(), P(), P())
    out_specs = P(("crop", "res"), None, None)
    return jax.shard_map(body, mesh=mesh, in_specs=in_specs, out_specs=out_specs, check_vma=False)
```

profile of v0, /device:TPU:1, one launch (start us, length us, event | category | flops | bytes accessed | tf_op | source)
XLA Modules:
  0.0 306.3 jit_solution(9634260150523408771)
XLA Ops:
  6.5 0.0 copy-start
  6.5 0.0 all-gather.2.cloned.1.call-start
  6.6 1.4 copy.38
  8.0 0.5 broadcast.38
  8.5 2.2 reduce.2
  10.8 0.2 reshape.58
  10.9 30.0 %all_to_all.4 = bf16[128,2,512]{2,1,0:T(2,128)(2,1)S(1)} all-to-all(bf16[128,2,512]{2,1,0:T(2,128)(2,1)S(1)} %reshape.58), channel_id=1, replica_groups=mesh['crop'=4,'res'=128] {'res'}, dimensions={0} | all-to-all | bytes 524288 | tf_op jit(solution)/shard_map/all_to_all | solution.py:49
  40.9 0.2 reshape.59
  41.2 0.1 convert_reduce_fusion
  41.3 0.2 fusion.10
  41.6 0.0 copy-done.2
  41.6 0.2 fusion.8
  41.8 0.0 copy-done
  41.8 0.2 convolution_convert_fusion.1
  42.0 0.1 copy.25
  42.1 0.7 copy.26
  42.8 0.0 all-gather.2.cloned.1.call-update
  42.9 0.0 copy-done.1
  42.9 0.2 convolution_convert_fusion
  43.0 0.1 copy.27
  43.2 0.1 reshape_reshape.3
  43.3 211.7 %all-gather.2.cloned.1.call-done = bf16[128,512,32]{0,2,1:T(8,128)(2,1)} async-done(((bf16[128,4,32]{0,2,1:T(8,128)(2,1)}), bf16[128,512,32]{0,2,1:T(8,128)(2,1)}) %all-gather.2.cloned.1.call-update) | async-done | bytes 4194320 | tf_op jit(solution)/shard_map/all_gather | solution.py:58
  255.1 43.6 %while.10 = (s32[]{:T(128)}, bf16[4,4,128,128]{3,2,1,0:T(8,128)(2,1)S(1)}, bf16[4,128,128,32]{1,3,2,0:T(8,128)(2,1)}, bf16[128,128]{1,0:T(8,128)(2,1)S(1)}, bf16...) while((s32[]{:T(128)}, bf16[4,4,128,128]{3,2,1,0:T(8,128)(2,1)S(1)}, ...), condition=%wide.region_3.4_spmd, body=%wide.region_2.3_spmd.sunk | while | flops 269615104 | bytes 12223061 | solution.py:83
  255.1 1.3 constant_dynamic-slice_fusion.2
  256.4 0.4 fusion.28
  256.8 0.5 copy.43
  257.3 4.4 %reshape.61 = bf16[4,32,128,32]{3,2,1,0:T(8,128)(2,1)} reshape(bf16[128,4096]{1,0:T(8,128)(2,1)S(1)} %copy.43) | data formatting | bytes 2097152 | tf_op jit(solution)/shard_map/while/body/eval_jaxpr/reshape | solution.py:71
  261.8 3.7 %copy.44 = bf16[4,128,32,32]{1,0,3,2:T(4,128)(2,1)S(1)} copy(bf16[4,128,32,32]{3,1,2,0:T(8,128)(2,1)} %bitcast.57) | data formatting | bytes 2097152 | tf_op jit(solution)/shard_map/while/body/eval_jaxpr/transpose | solution.py:74
  265.4 0.5 fusion.29
  266.0 1.3 constant_dynamic-slice_fusion.2
  267.3 0.4 fusion.28
  267.7 0.5 copy.43
  268.2 4.4 %reshape.61 = bf16[4,32,128,32]{3,2,1,0:T(8,128)(2,1)} reshape(bf16[128,4096]{1,0:T(8,128)(2,1)S(1)} %copy.43) | data formatting | bytes 2097152 | tf_op jit(solution)/shard_map/while/body/eval_jaxpr/reshape | solution.py:71
  272.7 3.7 %copy.44 = bf16[4,128,32,32]{1,0,3,2:T(4,128)(2,1)S(1)} copy(bf16[4,128,32,32]{3,1,2,0:T(8,128)(2,1)} %bitcast.57) | data formatting | bytes 2097152 | tf_op jit(solution)/shard_map/while/body/eval_jaxpr/transpose | solution.py:74
  276.3 0.5 fusion.29
  276.9 1.3 constant_dynamic-slice_fusion.2
  278.2 0.4 fusion.28
  278.6 0.5 copy.43
  279.1 4.4 %reshape.61 = bf16[4,32,128,32]{3,2,1,0:T(8,128)(2,1)} reshape(bf16[128,4096]{1,0:T(8,128)(2,1)S(1)} %copy.43) | data formatting | bytes 2097152 | tf_op jit(solution)/shard_map/while/body/eval_jaxpr/reshape | solution.py:71
  283.6 3.7 %copy.44 = bf16[4,128,32,32]{1,0,3,2:T(4,128)(2,1)S(1)} copy(bf16[4,128,32,32]{3,1,2,0:T(8,128)(2,1)} %bitcast.57) | data formatting | bytes 2097152 | tf_op jit(solution)/shard_map/while/body/eval_jaxpr/transpose | solution.py:74
  287.2 0.5 fusion.29
  287.8 1.3 constant_dynamic-slice_fusion.2
  289.1 0.4 fusion.28
  289.5 0.5 copy.43
  290.0 4.4 %reshape.61 = bf16[4,32,128,32]{3,2,1,0:T(8,128)(2,1)} reshape(bf16[128,4096]{1,0:T(8,128)(2,1)S(1)} %copy.43) | data formatting | bytes 2097152 | tf_op jit(solution)/shard_map/while/body/eval_jaxpr/reshape | solution.py:71
  294.5 3.7 %copy.44 = bf16[4,128,32,32]{1,0,3,2:T(4,128)(2,1)S(1)} copy(bf16[4,128,32,32]{3,1,2,0:T(8,128)(2,1)} %bitcast.57) | data formatting | bytes 2097152 | tf_op jit(solution)/shard_map/while/body/eval_jaxpr/transpose | solution.py:74
  298.1 0.5 fusion.29
  298.7 0.8 copy.28
  (13 shorter events, 0.1 us)
Async XLA Ops:
  6.5 35.3 %copy-start = (bf16[256,32]{0,1:T(8,128)(2,1)S(1)}, bf16[256,32]{0,1:T(8,128)(2,1)}, u32[]{:S(2)}) copy-start(bf16[256,32]{0,1:T(8,128)(2,1)} %param.11) | copy-start | bytes 49156
  6.5 35.0 %copy-start.2 = (f32[256]{0:T(256)S(1)}, f32[256]{0:T(256)}, u32[]{:S(2)}) copy-start(f32[256]{0:T(256)} %param.9) | copy-start | bytes 3076
  6.5 36.3 %copy-start.1 = (bf16[256,32]{0,1:T(8,128)(2,1)S(1)}, bf16[256,32]{0,1:T(8,128)(2,1)}, u32[]{:S(2)}) copy-start(bf16[256,32]{0,1:T(8,128)(2,1)} %param.10) | copy-start | bytes 49156
  6.5 248.5 %copy-start.3 = (bf16[1024,128]{1,0:T(8,128)(2,1)S(1)}, bf16[1024,128]{1,0:T(8,128)(2,1)}, u32[]{:S(2)}) copy-start(bf16[1024,128]{1,0:T(8,128)(2,1)} %param.12) | copy-start | bytes 786436
  6.5 248.5 %copy-start.4 = (f32[128]{0:T(128)S(1)}, f32[128]{0:T(128)}, u32[]{:S(2)}) copy-start(f32[128]{0:T(128)} %param.13) | copy-start | bytes 1540
  6.5 248.5 %all-gather.2.cloned.1.call-start = ((), (), s32[]{:S(2)}) async-start(), calls=%async_computation.1 | async-start | bytes 4227072 | tf_op jit(solution)/shard_map/all_gather | solution.py:58
Sparse Core Ops, SparseCore 0:
  43.0 212.0 all-gather.1
where the time goes:
time: 307 us; the launch traced here: 306 us
  waiting for transfers between devices  212 us (69%)
  local copies, waits for them, and re-layouts  44.1 us (14%)
  blocking collectives  30 us (10%)
  between operations  13.5 us (4%)
  matrix products  3.93 us (1%)
    all_gather x1, waiting for transfers between devices, body(): piece = lax.all_gather(second_factor, 'res', axis=1, tiled=True)  212 us
    all_to_all x1, blocking collectives, body(): lax.all_to_all(alignment_features, 'res', split_axis=1, concat_axis=0, ti...  30 us
    reshape x4, local copies, waits for them, and re-layouts, one_block(): tensor_products.astype(jnp.bfloat16)  17.8 us
    transpose x4, local copies, waits for them, and re-layouts, one_block(): tensor_products.transpose(0, 2, 1, 3)  14.6 us
  transfers between devices with their start and end apart: 1, of which 1 were waited for; matrix products, arithmetic and copies ran while one was open for 0% of the time, Pallas kernels for 0%

commit v1 on v0

v1 whole, which is shorter than its diff:
```python
import jax
import jax.numpy as jnp
from jax import lax
from jax.experimental import pallas as pl
from jax.experimental.pallas import tpu as pltpu
from jax.sharding import Mesh, PartitionSpec as P

Y, Z, X, C = 2, 8, 4, 2
F32, BF16 = jnp.float32, jnp.bfloat16
CHIP = ("y", "z", "x")
SLAB = ("y", "x", "c")
ALL = ("crop", "y", "z", "x", "c")


def project_kernel(x_ref, gain_ref, first_ref, second_ref, message_ref, rows_ref):
    x = x_ref[...].astype(F32)
    mean = jnp.mean(x, axis=-1, keepdims=True)
    centred = x - mean
    variance = jnp.mean(centred * centred, axis=-1, keepdims=True)
    normed = (centred * lax.rsqrt(variance + 1e-05) * gain_ref[...]).astype(BF16)
    first = first_ref[...]
    first4 = jnp.concatenate([first] * 4, axis=1)
    rows_ref[...] = jnp.dot(normed, first4, preferred_element_type=F32)
    group = lax.broadcasted_iota(jnp.int32, (128, 128), 1) // 32
    left = rows_ref[pl.ds(0, 128, stride=4), :]
    for r in range(1, 4):
        left = jnp.where(group == r, rows_ref[pl.ds(r, 128, stride=4), :], left)
    right = lax.dot_general(
        second_ref[...], normed, (((0,), (1,)), ((), ())), preferred_element_type=F32
    )
    low = lax.broadcasted_iota(jnp.int32, (16, 128), 1) < 64
    lefts = []
    for z in range(Z):
        lefts.append(
            jnp.concatenate([left[z * 8 : z * 8 + 8], left[64 + z * 8 : 72 + z * 8]], axis=0).astype(BF16)
        )
    for pair in range(4):
        head = right[:16, pair * 128 : pair * 128 + 128]
        tail = right[16:, pair * 128 : pair * 128 + 128]
        even = jnp.where(low, head, pltpu.roll(tail, 64, 1)).astype(BF16)
        odd = jnp.where(low, pltpu.roll(head, 64, 1), tail).astype(BF16)
        for which, block in ((2 * pair, even), (2 * pair + 1, odd)):
            y, xx = which // X, which % X
            for z in range(Z):
                at = (y * Z + z) * X + xx
                message_ref[at, :16, :] = lefts[z]
                message_ref[at, 16:, :] = block


def pair_kernel(core_ref, own_ref, other_ref, mix_ref, offset_ref, out_ref, flat_ref, wide_ref, lhs_ref, right_ref, outer_ref):
    core = core_ref[0]
    wide_ref[...] = mix_ref[...].astype(F32)
    mixer = jnp.concatenate(
        [wide_ref[pl.ds(e, 32, stride=32), :] for e in range(32)], axis=0
    ).T.astype(BF16)
    flat_ref[: 64 * 32] = own_ref[...].astype(F32).reshape(64 * 32, 128)
    flat_ref[64 * 32 :] = other_ref[...].astype(F32).reshape(64 * 32, 128)
    for row in range(16):
        block = flat_ref[pl.ds(row, 128, stride=32), :].T
        half = jnp.where(core == 0, block[:64], block[64:]).astype(BF16)
        lhs_ref[row * 32 : row * 32 + 32, :128] = half[:32]
        lhs_ref[row * 32 : row * 32 + 32, 128:] = half[32:]
    low = lax.broadcasted_iota(jnp.int32, (128, 128), 1) < 64
    zero = jnp.zeros((128, 128), F32)
    for row in range(16):
        block = flat_ref[pl.ds(16 + row, 128, stride=32), :]
        rolled = pltpu.roll(block, 64, 1)
        for e, lower, upper in ((row, block, rolled), (row + 16, rolled, block)):
            right_ref[:128, e * 128 : e * 128 + 128] = jnp.where(low, lower, zero).astype(BF16)
            right_ref[128:, e * 128 : e * 128 + 128] = jnp.where(low, zero, upper).astype(BF16)
    for pair in range(16):
        product = jnp.dot(
            lhs_ref[...], right_ref[:, pair * 256 : pair * 256 + 256], preferred_element_type=F32
        ).astype(BF16)
        for half in range(2):
            e = pair * 2 + half
            for row in range(16):
                outer_ref[e * 32 : e * 32 + 32, row * 128 : row * 128 + 128] = product[
                    row * 32 : row * 32 + 32, half * 128 : half * 128 + 128
                ]
    for pair in range(8):
        result = jnp.dot(
            mixer, outer_ref[:, pair * 256 : pair * 256 + 256], preferred_element_type=F32
        )
        for half in range(2):
            block = result[:, half * 128 : half * 128 + 128].T
            out_ref[pair * 2 + half] = (block * (1.0 / 128) + offset_ref[...]).astype(BF16)


def body(x, gain, first, second, mix, offset):
    x = x.reshape(512, 256)
    message = pl.pallas_call(
        project_kernel,
        out_shape=jax.ShapeDtypeStruct((64, 32, 128), BF16),
        scratch_shapes=[pltpu.VMEM((512, 128), F32)],
        compiler_params=pltpu.CompilerParams(vmem_limit_bytes=32 * 1024 * 1024),
    )(x, gain.reshape(1, 256), first, second)
    own = lax.all_to_all(message, CHIP, split_axis=0, concat_axis=0, tiled=True)
    other = lax.ppermute(own, "c", [(0, 1), (1, 0)])
    core = lax.axis_index("c").reshape(1)
    vmem = pl.BlockSpec(memory_space=pltpu.VMEM)
    tile = pl.pallas_call(
        pair_kernel,
        out_shape=jax.ShapeDtypeStruct((16, 128, 128), BF16),
        in_specs=[pl.BlockSpec(memory_space=pltpu.SMEM)] + [vmem] * 4,
        out_specs=vmem,
        scratch_shapes=[
            pltpu.VMEM((128 * 32, 128), F32),
            pltpu.VMEM((1024, 128), F32),
            pltpu.VMEM((512, 256), BF16),
            pltpu.VMEM((256, 4096), BF16),
            pltpu.VMEM((1024, 2048), BF16),
        ],
        compiler_params=pltpu.CompilerParams(vmem_limit_bytes=48 * 1024 * 1024),
    )(core, own, other, mix, offset.reshape(1, 128))
    got = lax.all_to_all(tile, SLAB, split_axis=0, concat_axis=0, tiled=True)
    got = got.reshape(Y, X, C, 2, 64, 128).transpose(2, 3, 0, 1, 4, 5)
    return got.reshape(4, 512, 128)


def solution(mesh):
    fine = Mesh(mesh.devices.reshape(mesh.devices.shape[0], Y, Z, X, C), ALL)
    split = P(ALL, None, None)
    return jax.shard_map(
        body, mesh=fine, in_specs=(split, P(), P(), P(), P(), P()), out_specs=split, check_vma=False
    )
```

time: 307 us -> 59.3 us (0.19)
  waiting for transfers between devices: 212 us -> 1.51 us
  local copies, waits for them, and re-layouts: 44.1 us -> 4.09 us
  between operations: 13.5 us -> 0.06 us
  blocking collectives: 30 us -> 43 us
  starting transfers between devices: 0.04 us -> 5.81 us
  Pallas kernels: 0 us -> 4.58 us
  matrix products: 3.93 us -> 0 us
    all_gather x1 -> x0, waiting for transfers between devices: 212 us -> none  [body(): piece = lax.all_gather(second_factor, 'res', axis=1, tiled=True)]
    reshape x5 -> x0, local copies, waits for them, and re-layouts: 18.5 us -> none  [the longest x4 17.8 us: one_block(): tensor_products.astype(jnp.bfloat16)]
    transpose x5 -> x1, local copies, waits for them, and re-layouts: 15.4 us -> 0.84 us  [body(): got = got.reshape(Y, X, C, 2, 64, 128).transpose(2, 3, 0, 1, 4, 5)]
    all_to_all x1 -> x2, blocking collectives: 30 us -> 43 us  [the longest x1 28.3 us: body(): own = lax.all_to_all(message, CHIP, split_axis=0, concat_axis=0, tiled=True)]
    ppermute x0 -> x1, starting transfers between devices: none -> 5.81 us  [body(): other = lax.ppermute(own, 'c', [(0, 1), (1, 0)])]
    dynamic_slice x4 -> x0, local copies, waits for them, and re-layouts: 5.18 us -> none  [body(): stacked = lax.map(one_block, grouped)]
    pallas_call x0 -> x2, Pallas kernels: none -> 4.58 us  [the longest x1 3.79 us: body(): pl.pallas_call(pair_kernel, out_shape=jax.ShapeDtypeStruct((16, 128, 128)...]
    dot_general x10 -> x0, matrix products: 3.93 us -> none  [the longest x4 1.91 us: one_block(): jnp.dot(tensor_products, final_mixing_matrix, preferred_element_type=jnp....]
where the time goes in v1:
time: 59.3 us; the launch traced here: 59 us
  blocking collectives  43 us (73%)
  starting transfers between devices  5.81 us (10%)
  Pallas kernels  4.58 us (8%)
  local copies, waits for them, and re-layouts  4.09 us (7%)
  waiting for transfers between devices  1.51 us (3%)
    all_to_all x1, blocking collectives, body(): own = lax.all_to_all(message, CHIP, split_axis=0, concat_axis=0, tiled=True)  28.3 us
    all_to_all x1, blocking collectives, body(): got = lax.all_to_all(tile, SLAB, split_axis=0, concat_axis=0, tiled=True)  14.7 us
    ppermute x1, starting transfers between devices, body(): other = lax.ppermute(own, 'c', [(0, 1), (1, 0)])  5.81 us
    pallas_call x1, Pallas kernels, body(): pl.pallas_call(pair_kernel, out_shape=jax.ShapeDtypeStruct((16, 128, 128)...  3.79 us
    unnamed x12, local copies, waits for them, and re-layouts  3.25 us
    ppermute x1, waiting for transfers between devices, body(): other = lax.ppermute(own, 'c', [(0, 1), (1, 0)])  1.51 us
  transfers between devices with their start and end apart: 1, of which 1 were waited for; matrix products, arithmetic and copies ran while one was open for 0% of the time, Pallas kernels for 0%

profile of v1, /device:TPU:1, one launch (start us, length us, event | category | flops | bytes accessed | tf_op | source)
XLA Modules:
  0.0 59.0 jit_solution(1661359781153074532)
XLA Ops:
  0.0 0.0 copy-start.4
  0.0 0.8 %copy.7.first_ref = bf16[256,32]{1,0:T(8,128)(2,1)S(1)} copy(bf16[256,32]{0,1:T(8,128)(2,1)} %param.8) | data formatting | bytes 32768 | tf_op args[2]
  0.9 0.0 copy-done.4
  0.9 0.1 copy.8.second_ref
  1.0 0.0 copy-start.2
  1.0 0.7 %copy-done.2 = f32[256]{0:T(256)S(1)} copy-done((f32[256]{0:T(256)S(1)}, f32[256]{0:T(256)}, u32[]{:S(2)}) %copy-start.2) | copy-done | bytes 1048
  1.7 0.0 copy-start.1
  1.7 0.9 %copy-done.1 = bf16[1,512,256]{2,1,0:T(8,128)(2,1)S(1)} copy-done((bf16[1,512,256]{2,1,0:T(8,128)(2,1)S(1)}, bf16[1,512,256]{2,1,0:T(8,128)(2,1)}, u32[]{:S(2)}) %copy-start.1) | copy-done | bytes 262168
  2.6 0.8 %shard_map.64 = bf16[64,32,128]{2,1,0:T(8,128)(2,1)S(1)} custom-call(bf16[512,256]{1,0:T(8,128)(2,1)S(1)} %bitcast.8, f32[1,256]{1,0:T(1,128)S(1)} %bitcast.9, bf16[256,32]{1,0:T(8,128)(2,1)S(1)} %copy.7.first_ref, bf16[256,32]{1,0:T(8,128)(2,1)S(1)} %copy.8.second_ref), custom_call_target="tpu_custom_call" | custom-call | tf_op jit(solution)/shard_map/pallas_call | solution.py:92
  3.4 0.0 copy-start
  3.4 28.3 %all_to_all.10.own_ref = bf16[64,32,128]{2,1,0:T(8,128)(2,1)S(1)} all-to-all(bf16[64,32,128]{2,1,0:T(8,128)(2,1)S(1)} %shard_map.64), channel_id=1, replica_groups=mesh['crop'=4,'y'=2,'z'=8,'x'=4,'c'=2] {'y','z','x'}, dimensions={0} | all-to-all | bytes 1048576 | tf_op jit(solution)/shard_map/all_to_all | solution.py:98
  31.7 5.8 %collective-permute-start = (bf16[64,32,128]{2,1,0:T(8,128)(2,1)S(1)}, bf16[64,32,128]{2,1,0:T(8,128)(2,1)S(1)}, u32[]{:S(2)}, u32[]{:S(2)}) collective-permute-start(bf16[64,32,128]{2,1,0:T(8,128)(2,1)S(1)} %all_to_all.10.own_ref), channel_id=1, source_target_pairs={{0,1},{1,0},{2,3},{3,2},{4,5},{5,4},{6,7},{7,6},{8,9},{9,8},{10,11... | collective-permute-start | bytes 1572872 | tf_op jit(solution)/shard_map/ppermute | solution.py:99
  37.5 1.5 %collective-permute-done.other_ref = bf16[64,32,128]{2,1,0:T(8,128)(2,1)S(1)} collective-permute-done((bf16[64,32,128]{2,1,0:T(8,128)(2,1)S(1)}, bf16[64,32,128]{2,1,0:T(8,128)(2,1)S(1)}, u32[]{:S(2)}, u32[]{:S(2)}) %collective-permute-start) | collective-permute-done | bytes 524320 | tf_op jit(solution)/shard_map/ppermute | solution.py:99
  39.1 0.0 copy-start.3
  39.1 0.0 copy-done
  39.1 0.7 %copy-done.3 = f32[128]{0:T(128)S(1)} copy-done((f32[128]{0:T(128)S(1)}, f32[128]{0:T(128)}, u32[]{:S(2)}) %copy-start.3) | copy-done | bytes 536
  39.7 3.8 %shard_map.65 = bf16[16,128,128]{2,1,0:T(8,128)(2,1)S(1)} custom-call(s32[1]{0:T(128)} %bitcast.core_ref, bf16[64,32,128]{2,1,0:T(8,128)(2,1)S(1)} %all_to_all.10.own_ref, bf16[64,32,128]{2,1,0:T(8,128)(2,1)S(1)} %collective-permute-done.other_ref, bf16[1024,128]{1,0:T(8,128)(2,1)S(1)} %copy-done, f32[1,128]{1,0:T(1,128)S(1)} %bitcast.10), custom_call_target="tpu_custom_call" | custom-call | tf_op jit(solution)/shard_map/pallas_call | solution.py:102
  43.5 14.7 %all_to_all.11 = bf16[16,128,128]{2,1,0:T(8,128)(2,1)S(1)} all-to-all(bf16[16,128,128]{2,1,0:T(8,128)(2,1)S(1)} %shard_map.65), channel_id=1, replica_groups=mesh['crop'=4,'y'=2,'z'=8,'x'=4,'c'=2] {'y','x','c'}, dimensions={0} | all-to-all | bytes 1048576 | tf_op jit(solution)/shard_map/all_to_all | solution.py:116
  58.2 0.8 %copy.9 = bf16[2,2,2,4,64,128]{5,4,3,2,1,0:T(8,128)(2,1)} copy(bf16[2,2,2,4,64,128]{5,4,1,0,3,2:T(8,128)(2,1)S(1)} %bitcast.11) | data formatting | bytes 1048576 | tf_op jit(solution)/shard_map/transpose | solution.py:117
Async XLA Ops:
  0.0 0.9 %copy-start.4 = (bf16[256,32]{0,1:T(8,128)(2,1)S(1)}, bf16[256,32]{0,1:T(8,128)(2,1)}, u32[]{:S(2)}) copy-start(bf16[256,32]{0,1:T(8,128)(2,1)} %param.9) | copy-start | bytes 49156
  1.0 0.7 %copy-start.2 = (f32[256]{0:T(256)S(1)}, f32[256]{0:T(256)}, u32[]{:S(2)}) copy-start(f32[256]{0:T(256)} %param.7) | copy-start | bytes 3076
  1.7 0.9 %copy-start.1 = (bf16[1,512,256]{2,1,0:T(8,128)(2,1)S(1)}, bf16[1,512,256]{2,1,0:T(8,128)(2,1)}, u32[]{:S(2)}) copy-start(bf16[1,512,256]{2,1,0:T(8,128)(2,1)} %param.6) | copy-start | bytes 786436
  3.4 35.7 %copy-start = (bf16[1024,128]{1,0:T(8,128)(2,1)S(1)}, bf16[1024,128]{1,0:T(8,128)(2,1)}, u32[]{:S(2)}) copy-start(bf16[1024,128]{1,0:T(8,128)(2,1)} %mix_ref.1) | copy-start | bytes 786436
  31.7 7.3 %collective-permute-start = (bf16[64,32,128]{2,1,0:T(8,128)(2,1)S(1)}, bf16[64,32,128]{2,1,0:T(8,128)(2,1)S(1)}, u32[]{:S(2)}, u32[]{:S(2)}) collective-permute-start(bf16[64,32,128]{2,1,0:T(8,128)(2,1)S(1)} %all_to_all.10.own_ref), channel_id=1, source_target_pairs={{0,1},{1,0},{2,3},{3,2},{4,5},{5,4},{6,7},{7,6},{8,9},{9,8},{10,11... | collective-permute-start | bytes 1572872 | tf_op jit(solution)/shard_map/ppermute | solution.py:99
  39.1 0.7 %copy-start.3 = (f32[128]{0:T(128)S(1)}, f32[128]{0:T(128)}, u32[]{:S(2)}) copy-start(f32[128]{0:T(128)} %param.11) | copy-start | bytes 1540

commit v2 on v1

v2 whole, which is shorter than its diff:
```python
import jax
import jax.numpy as jnp
from jax import lax
from jax.experimental import pallas as pl
from jax.experimental.pallas import tpu as pltpu
from jax.sharding import Mesh, PartitionSpec as P

Y, Z, X, C = 2, 8, 4, 2
F32, BF16 = jnp.float32, jnp.bfloat16
CHIP = ("y", "z", "x")
COLUMN = ("y", "x")
ALL = ("crop", "y", "z", "x", "c")
NT = (((1,), (1,)), ((), ()))
MIB = 1024 * 1024


def project_kernel(x_hbm, gain_hbm, first_hbm, second_hbm, message_ref, x_ref, gain_ref, first_ref, second_ref, rows_ref, sems):
    small = [
        pltpu.make_async_copy(gain_hbm, gain_ref, sems.at[4]),
        pltpu.make_async_copy(first_hbm, first_ref, sems.at[5]),
        pltpu.make_async_copy(second_hbm, second_ref, sems.at[6]),
    ]
    chunks = [
        pltpu.make_async_copy(x_hbm.at[pl.ds(k * 128, 128)], x_ref.at[pl.ds(k * 128, 128)], sems.at[k])
        for k in range(4)
    ]
    for copy in [chunks[0]] + small + chunks[1:]:
        copy.start()
    low = lax.broadcasted_iota(jnp.int32, (16, 128), 1) < 64
    for k in range(4):
        chunks[k].wait()
        if k == 0:
            for copy in small:
                copy.wait()
            first4 = jnp.concatenate([first_ref[...]] * 4, axis=0)
        x = x_ref[k * 128 : k * 128 + 128].astype(F32)
        mean = jnp.mean(x, axis=-1, keepdims=True)
        centred = x - mean
        variance = jnp.mean(centred * centred, axis=-1, keepdims=True)
        normed = (centred * lax.rsqrt(variance + 1e-05) * gain_ref[...]).astype(BF16)
        rows_ref[k * 128 : k * 128 + 128] = lax.dot_general(normed, first4, NT, preferred_element_type=F32)
        right = lax.dot_general(second_ref[...], normed, NT, preferred_element_type=F32)
        head, tail = right[:16], right[16:]
        even = jnp.where(low, head, pltpu.roll(tail, 64, 1)).astype(BF16)
        odd = jnp.where(low, pltpu.roll(head, 64, 1), tail).astype(BF16)
        for which, block in ((2 * k, even), (2 * k + 1, odd)):
            for z in range(Z):
                message_ref[(which // X * Z + z) * X + which % X, 16:, :] = block
    group = lax.broadcasted_iota(jnp.int32, (128, 128), 1) // 32
    left = rows_ref[pl.ds(0, 128, stride=4), :]
    for r in range(1, 4):
        left = jnp.where(group == r, rows_ref[pl.ds(r, 128, stride=4), :], left)
    for z in range(Z):
        block = jnp.concatenate([left[z * 8 : z * 8 + 8], left[64 + z * 8 : 72 + z * 8]], axis=0).astype(BF16)
        for y in range(Y):
            for xx in range(X):
                message_ref[(y * Z + z) * X + xx, :16, :] = block


def spread(core, half_ref, flat_ref, lhs_ref, right_ref):
    flat_ref[...] = half_ref[...].astype(F32).reshape(64 * 32, 128)
    for owner in range(8):
        block = flat_ref[pl.ds(owner * 2 + core, 64, stride=32), :]
        both = jnp.concatenate([block, pltpu.roll(block, 96, 1)], axis=0).T.astype(BF16)
        lhs_ref[owner * 64 : owner * 64 + 32] = both[:32]
        lhs_ref[owner * 64 + 32 : owner * 64 + 64] = both[64:96]
    low = lax.broadcasted_iota(jnp.int32, (64, 128), 1) < 64
    zero = jnp.zeros((64, 128), F32)
    for row in range(16):
        block = flat_ref[pl.ds(16 + row, 64, stride=32), :]
        rolled = pltpu.roll(block, 64, 1)
        for e, lower, upper in ((row, block, rolled), (row + 16, rolled, block)):
            right_ref[:64, e * 128 : e * 128 + 128] = jnp.where(low, lower, zero).astype(BF16)
            right_ref[64:, e * 128 : e * 128 + 128] = jnp.where(low, zero, upper).astype(BF16)


def own_kernel(core_ref, own_ref, mix_ref, lhs_ref, right_ref, mixer_ref, flat_ref, wide_ref):
    wide_ref[...] = mix_ref[...].astype(F32)
    for e in range(0, 32, 4):
        rows = [wide_ref[pl.ds(e + k, 32, stride=32), :] for k in range(4)]
        mixer_ref[:, e * 32 : e * 32 + 128] = jnp.concatenate(rows, axis=0).T.astype(BF16)
    spread(core_ref[0], own_ref, flat_ref, lhs_ref, right_ref)


def pair_kernel(core_ref, other_ref, lhs_ref, right_ref, mixer_ref, offset_hbm, out_ref, flat_ref, lhs2_ref, right2_ref, outer_ref, offset_ref, sem):
    copy = pltpu.make_async_copy(offset_hbm, offset_ref, sem)
    copy.start()
    spread(core_ref[0], other_ref, flat_ref, lhs2_ref, right2_ref)
    lhs = jnp.concatenate([lhs_ref[...], lhs2_ref[...]], axis=1)
    for pair in range(16):
        at = slice(pair * 256, pair * 256 + 256)
        right = jnp.concatenate([right_ref[:, at], right2_ref[:, at]], axis=0)
        product = jnp.dot(lhs, right, preferred_element_type=F32).astype(BF16)
        for half in range(2):
            e = pair * 2 + half
            for row in range(16):
                outer_ref[e * 32 : e * 32 + 32, row * 128 : row * 128 + 128] = product[
                    row * 32 : row * 32 + 32, half * 128 : half * 128 + 128
                ]
    copy.wait()
    offset = offset_ref[...]
    for pair in range(8):
        result = jnp.dot(
            mixer_ref[...], outer_ref[:, pair * 256 : pair * 256 + 256], preferred_element_type=F32
        )
        for half in range(2):
            block = result[:, half * 128 : half * 128 + 128].T
            out_ref[pair * 2 + half] = (block * (1.0 / 128) + offset).astype(BF16)


def in_hbm(array):
    return pltpu.with_memory_space_constraint(array, pltpu.HBM)


def body(x, gain, first, second, mix, offset):
    hbm = pl.BlockSpec(memory_space=pltpu.HBM)
    vmem = pl.BlockSpec(memory_space=pltpu.VMEM)
    smem = pl.BlockSpec(memory_space=pltpu.SMEM)
    message = pl.pallas_call(
        project_kernel,
        out_shape=jax.ShapeDtypeStruct((64, 32, 128), BF16),
        in_specs=[hbm] * 4,
        out_specs=vmem,
        scratch_shapes=[
            pltpu.VMEM((512, 256), BF16),
            pltpu.VMEM((1, 256), F32),
            pltpu.VMEM((32, 256), BF16),
            pltpu.VMEM((32, 256), BF16),
            pltpu.VMEM((512, 128), F32),
            pltpu.SemaphoreType.DMA((7,)),
        ],
        compiler_params=pltpu.CompilerParams(vmem_limit_bytes=32 * MIB),
    )(in_hbm(x.reshape(512, 256)), in_hbm(gain.reshape(1, 256)), in_hbm(first.T), in_hbm(second.T))
    own = lax.all_to_all(message, CHIP, split_axis=0, concat_axis=0, tiled=True)
    other = lax.ppermute(own, "c", [(0, 1), (1, 0)])
    core = lax.axis_index("c").reshape(1)
    lhs, right, mixer = pl.pallas_call(
        own_kernel,
        out_shape=(
            jax.ShapeDtypeStruct((512, 128), BF16),
            jax.ShapeDtypeStruct((128, 4096), BF16),
            jax.ShapeDtypeStruct((128, 1024), BF16),
        ),
        in_specs=[smem, vmem, vmem],
        out_specs=(vmem, vmem, vmem),
        scratch_shapes=[pltpu.VMEM((64 * 32, 128), F32), pltpu.VMEM((1024, 128), F32)],
        compiler_params=pltpu.CompilerParams(vmem_limit_bytes=32 * MIB),
        cost_estimate=pl.CostEstimate(flops=2_000_000, bytes_accessed=2_000_000, transcendentals=0),
    )(core, own, mix)
    tile = pl.pallas_call(
        pair_kernel,
        out_shape=jax.ShapeDtypeStruct((16, 128, 128), BF16),
        in_specs=[smem, vmem, vmem, vmem, vmem, hbm],
        out_specs=vmem,
        scratch_shapes=[
            pltpu.VMEM((64 * 32, 128), F32),
            pltpu.VMEM((512, 128), BF16),
            pltpu.VMEM((128, 4096), BF16),
            pltpu.VMEM((1024, 2048), BF16),
            pltpu.VMEM((1, 128), F32),
            pltpu.SemaphoreType.DMA,
        ],
        compiler_params=pltpu.CompilerParams(vmem_limit_bytes=32 * MIB),
    )(core, other, lhs, right, mixer, in_hbm(offset.reshape(1, 128)))
    tile = tile.reshape(8, 4, 64, 128)
    got = lax.all_to_all(tile, COLUMN, split_axis=0, concat_axis=0, tiled=True)
    return got.transpose(1, 0, 2, 3).reshape(4, 512, 128)


def solution(mesh):
    fine = Mesh(mesh.devices.reshape(mesh.devices.shape[0], Y, Z, X, C), ALL)
    split = P(ALL, None, None)
    return jax.shard_map(
        body, mesh=fine, in_specs=(split, P(), P(), P(), P(), P()), out_specs=split, check_vma=False
    )
```

time: 59.3 us -> 56.2 us (0.948); the launches traced: 59 us -> 55.3 us
  local copies, waits for them, and re-layouts: 4.09 us -> 0.84 us
  Pallas kernels: 4.58 us -> 6.95 us
  blocking collectives: 43 us -> 41.3 us
  waiting for transfers between devices: 1.51 us -> 0.32 us
    unnamed x12 -> x2, local copies, waits for them, and re-layouts: 3.25 us -> 0.01 us
    pallas_call x1, Pallas kernels: 0.79 us -> 2.5 us  [body(): pl.pallas_call(project_kernel, out_shape=jax.ShapeDtypeStruct((64, 32, 12...]
    all_to_all x1, blocking collectives: 14.7 us -> 13 us  [body(): got = lax.all_to_all(tile, COLUMN, split_axis=0, concat_axis=0, tiled=True)]
    ppermute x1, waiting for transfers between devices: 1.51 us -> 0.32 us  [body(): other = lax.ppermute(own, 'c', [(0, 1), (1, 0)])]
    pallas_call x0 -> x1, Pallas kernels: none -> 1.17 us  [body(): pl.pallas_call(own_kernel, out_shape=(jax.ShapeDtypeStruct((512, 128), BF...]
  transfers between devices with their start and end apart: 1 -> 1, of which waited for: 1 -> 1; matrix products, arithmetic and copies ran while one was open for 0% -> 0% of each run, Pallas kernels for 0% -> 2%
where the time goes in v2:
time: 56.2 us; the launch traced here: 55.3 us
  blocking collectives  41.3 us (73%)
  Pallas kernels  6.95 us (12%)
  starting transfers between devices  5.81 us (10%)
  local copies, waits for them, and re-layouts  0.84 us (1%)
    all_to_all x1, blocking collectives, body(): own = lax.all_to_all(message, CHIP, split_axis=0, concat_axis=0, tiled=True)  28.3 us
    all_to_all x1, blocking collectives, body(): got = lax.all_to_all(tile, COLUMN, split_axis=0, concat_axis=0, tiled=True)  13 us
    ppermute x1, starting transfers between devices, body(): other = lax.ppermute(own, 'c', [(0, 1), (1, 0)])  5.81 us
    pallas_call x1, Pallas kernels, body(): pl.pallas_call(pair_kernel, out_shape=jax.ShapeDtypeStruct((16, 128, 128)...  3.28 us
    pallas_call x1, Pallas kernels, body(): pl.pallas_call(project_kernel, out_shape=jax.ShapeDtypeStruct((64, 32, 12...  2.5 us
    pallas_call x1, Pallas kernels, body(): pl.pallas_call(own_kernel, out_shape=(jax.ShapeDtypeStruct((512, 128), BF...  1.17 us
  transfers between devices with their start and end apart: 1, of which 1 were waited for; matrix products, arithmetic and copies ran while one was open for 0% of the time, Pallas kernels for 2%

profile of v2, /device:TPU:1, one launch (start us, length us, event | category | flops | bytes accessed | tf_op | source)
XLA Modules:
  0.0 55.3 jit_solution(3144535081749191146)
XLA Ops:
  0.0 2.5 %shard_map.64 = bf16[64,32,128]{2,1,0:T(8,128)(2,1)S(1)} custom-call(bf16[512,256]{1,0:T(8,128)(2,1)} %bitcast.11, f32[1,256]{1,0:T(1,128)} %bitcast.14, bf16[32,256]{1,0:T(8,128)(2,1)} %bitcast.12, bf16[32,256]{1,0:T(8,128)(2,1)} %bitcast.13), custom_call_target="tpu_custom_call" | custom-call | tf_op jit(solution)/shard_map/pallas_call | solution.py:119
  2.5 0.0 copy-start
  2.5 28.3 %all_to_all.10.own_ref = bf16[64,32,128]{2,1,0:T(8,128)(2,1)S(1)} all-to-all(bf16[64,32,128]{2,1,0:T(8,128)(2,1)S(1)} %shard_map.64), channel_id=1, replica_groups=mesh['crop'=4,'y'=2,'z'=8,'x'=4,'c'=2] {'y','z','x'}, dimensions={0} | all-to-all | bytes 1048576 | tf_op jit(solution)/shard_map/all_to_all | solution.py:134
  30.8 5.8 %collective-permute-start = (bf16[64,32,128]{2,1,0:T(8,128)(2,1)S(1)}, bf16[64,32,128]{2,1,0:T(8,128)(2,1)S(1)}, u32[]{:S(2)}, u32[]{:S(2)}) collective-permute-start(bf16[64,32,128]{2,1,0:T(8,128)(2,1)S(1)} %all_to_all.10.own_ref), channel_id=1, source_target_pairs={{0,1},{1,0},{2,3},{3,2},{4,5},{5,4},{6,7},{7,6},{8,9},{9,8},{10,11... | collective-permute-start | bytes 1572872 | tf_op jit(solution)/shard_map/ppermute | solution.py:135
  36.7 0.0 copy-done
  36.7 1.2 %shard_map.65 = (bf16[512,128]{1,0:T(8,128)(2,1)S(1)}, bf16[128,4096]{1,0:T(8,128)(2,1)S(1)}, bf16[128,1024]{1,0:T(8,128)(2,1)S(1)}) custom-call(s32[1]{0:T(128)} %bitcast.core_ref, bf16[64,32,128]{2,1,0:T(8,128)(2,1)S(1)} %all_to_all.10.own_ref, bf16[1024,128]{1,0:T(8,128)(2,1)S(1)} %copy-done), custom_call_target="tpu_custom_call" | custom-call | flops 2000000 | bytes 2000000 | tf_op jit(solution)/shard_map/pallas_call | solution.py:137
  37.8 0.3 collective-permute-done.other_ref
  38.2 3.3 %shard_map.66 = bf16[16,128,128]{2,1,0:T(8,128)(2,1)S(1)} custom-call(s32[1]{0:T(128)} %bitcast.core_ref, bf16[64,32,128]{2,1,0:T(8,128)(2,1)S(1)} %collective-permute-done.other_ref, bf16[512,128]{1,0:T(8,128)(2,1)S(1)} %get-tuple-element.8.lhs_ref, bf16[128,4096]{1,0:T(8,128)(2,1)S(1)} %get-tuple-element.9.right_ref, ...), custom_call_target="tpu_custom_call" | custom-call | tf_op jit(solution)/shard_map/pallas_call | solution.py:150
  41.4 13.0 %all_to_all.11 = bf16[8,4,64,128]{3,2,1,0:T(8,128)(2,1)S(1)} all-to-all(bf16[8,4,64,128]{3,2,1,0:T(8,128)(2,1)S(1)} %bitcast.9), channel_id=1, replica_groups=mesh['crop'=4,'y'=2,'z'=8,'x'=4,'c'=2] {'y','x'}, dimensions={0} | all-to-all | bytes 1048576 | tf_op jit(solution)/shard_map/all_to_all | solution.py:166
  54.5 0.8 %copy.7 = bf16[4,8,64,128]{3,2,1,0:T(8,128)(2,1)} copy(bf16[4,8,64,128]{3,2,0,1:T(8,128)(2,1)S(1)} %bitcast.10) | data formatting | bytes 1048576 | tf_op jit(solution)/shard_map/transpose | solution.py:167
Async XLA Ops:
  2.5 34.1 %copy-start = (bf16[1024,128]{1,0:T(8,128)(2,1)S(1)}, bf16[1024,128]{1,0:T(8,128)(2,1)}, u32[]{:S(2)}) copy-start(bf16[1024,128]{1,0:T(8,128)(2,1)} %mix_ref.1) | copy-start | bytes 786436
  30.8 7.3 %collective-permute-start = (bf16[64,32,128]{2,1,0:T(8,128)(2,1)S(1)}, bf16[64,32,128]{2,1,0:T(8,128)(2,1)S(1)}, u32[]{:S(2)}, u32[]{:S(2)}) collective-permute-start(bf16[64,32,128]{2,1,0:T(8,128)(2,1)S(1)} %all_to_all.10.own_ref), channel_id=1, source_target_pairs={{0,1},{1,0},{2,3},{3,2},{4,5},{5,4},{6,7},{7,6},{8,9},{9,8},{10,11... | collective-permute-start | bytes 1572872 | tf_op jit(solution)/shard_map/ppermute | solution.py:135

commit v3 on v2

--- a/solution.py
+++ b/solution.py
@@ -24,15 +24,13 @@
         pltpu.make_async_copy(x_hbm.at[pl.ds(k * 128, 128)], x_ref.at[pl.ds(k * 128, 128)], sems.at[k])
         for k in range(4)
     ]
-    for copy in [chunks[0]] + small + chunks[1:]:
+    for copy in chunks + small:
         copy.start()
+    for copy in chunks + small:
+        copy.wait()
     low = lax.broadcasted_iota(jnp.int32, (16, 128), 1) < 64
+    first4 = jnp.concatenate([first_ref[...]] * 4, axis=0)
     for k in range(4):
-        chunks[k].wait()
-        if k == 0:
-            for copy in small:
-                copy.wait()
-            first4 = jnp.concatenate([first_ref[...]] * 4, axis=0)
         x = x_ref[k * 128 : k * 128 + 128].astype(F32)
         mean = jnp.mean(x, axis=-1, keepdims=True)
         centred = x - mean

time: 56.2 us -> 55.3 us (0.984)
  Pallas kernels: 6.95 us -> 6.04 us
    pallas_call x1, Pallas kernels: 2.5 us -> 1.59 us  [body(): pl.pallas_call(project_kernel, out_shape=jax.ShapeDtypeStruct((64, 32, 12...]
where the time goes in v3:
time: 55.3 us; the launch traced here: 54.4 us
  blocking collectives  41.3 us (75%)
  Pallas kernels  6.04 us (11%)
  starting transfers between devices  5.81 us (11%)
  local copies, waits for them, and re-layouts  0.84 us (2%)
    all_to_all x1, blocking collectives, body(): own = lax.all_to_all(message, CHIP, split_axis=0, concat_axis=0, tiled=True)  28.3 us
    all_to_all x1, blocking collectives, body(): got = lax.all_to_all(tile, COLUMN, split_axis=0, concat_axis=0, tiled=True)  13 us
    ppermute x1, starting transfers between devices, body(): other = lax.ppermute(own, 'c', [(0, 1), (1, 0)])  5.81 us
    pallas_call x1, Pallas kernels, body(): pl.pallas_call(pair_kernel, out_shape=jax.ShapeDtypeStruct((16, 128, 128)...  3.28 us
    pallas_call x1, Pallas kernels, body(): pl.pallas_call(project_kernel, out_shape=jax.ShapeDtypeStruct((64, 32, 12...  1.59 us
    pallas_call x1, Pallas kernels, body(): pl.pallas_call(own_kernel, out_shape=(jax.ShapeDtypeStruct((512, 128), BF...  1.17 us
  transfers between devices with their start and end apart: 1, of which 1 were waited for; matrix products, arithmetic and copies ran while one was open for 0% of the time, Pallas kernels for 2%

profile of v3, /device:TPU:1, one launch (start us, length us, event | category | flops | bytes accessed | tf_op | source)
XLA Modules:
  0.0 54.4 jit_solution(18069368559297704588)
XLA Ops:
  0.0 1.6 %shard_map.64 = bf16[64,32,128]{2,1,0:T(8,128)(2,1)S(1)} custom-call(bf16[512,256]{1,0:T(8,128)(2,1)} %bitcast.11, f32[1,256]{1,0:T(1,128)} %bitcast.14, bf16[32,256]{1,0:T(8,128)(2,1)} %bitcast.12, bf16[32,256]{1,0:T(8,128)(2,1)} %bitcast.13), custom_call_target="tpu_custom_call" | custom-call | tf_op jit(solution)/shard_map/pallas_call | solution.py:117
  1.6 0.0 copy-start
  1.6 28.3 %all_to_all.10.own_ref = bf16[64,32,128]{2,1,0:T(8,128)(2,1)S(1)} all-to-all(bf16[64,32,128]{2,1,0:T(8,128)(2,1)S(1)} %shard_map.64), channel_id=1, replica_groups=mesh['crop'=4,'y'=2,'z'=8,'x'=4,'c'=2] {'y','z','x'}, dimensions={0} | all-to-all | bytes 1048576 | tf_op jit(solution)/shard_map/all_to_all | solution.py:132
  29.9 5.8 %collective-permute-start = (bf16[64,32,128]{2,1,0:T(8,128)(2,1)S(1)}, bf16[64,32,128]{2,1,0:T(8,128)(2,1)S(1)}, u32[]{:S(2)}, u32[]{:S(2)}) collective-permute-start(bf16[64,32,128]{2,1,0:T(8,128)(2,1)S(1)} %all_to_all.10.own_ref), channel_id=1, source_target_pairs={{0,1},{1,0},{2,3},{3,2},{4,5},{5,4},{6,7},{7,6},{8,9},{9,8},{10,11... | collective-permute-start | bytes 1572872 | tf_op jit(solution)/shard_map/ppermute | solution.py:133
  35.7 0.0 copy-done
  35.8 1.2 %shard_map.65 = (bf16[512,128]{1,0:T(8,128)(2,1)S(1)}, bf16[128,4096]{1,0:T(8,128)(2,1)S(1)}, bf16[128,1024]{1,0:T(8,128)(2,1)S(1)}) custom-call(s32[1]{0:T(128)} %bitcast.core_ref, bf16[64,32,128]{2,1,0:T(8,128)(2,1)S(1)} %all_to_all.10.own_ref, bf16[1024,128]{1,0:T(8,128)(2,1)S(1)} %copy-done), custom_call_target="tpu_custom_call" | custom-call | flops 2000000 | bytes 2000000 | tf_op jit(solution)/shard_map/pallas_call | solution.py:135
  36.9 0.3 collective-permute-done.other_ref
  37.3 3.3 %shard_map.66 = bf16[16,128,128]{2,1,0:T(8,128)(2,1)S(1)} custom-call(s32[1]{0:T(128)} %bitcast.core_ref, bf16[64,32,128]{2,1,0:T(8,128)(2,1)S(1)} %collective-permute-done.other_ref, bf16[512,128]{1,0:T(8,128)(2,1)S(1)} %get-tuple-element.8.lhs_ref, bf16[128,4096]{1,0:T(8,128)(2,1)S(1)} %get-tuple-element.9.right_ref, ...), custom_call_target="tpu_custom_call" | custom-call | tf_op jit(solution)/shard_map/pallas_call | solution.py:148
  40.5 13.0 %all_to_all.11 = bf16[8,4,64,128]{3,2,1,0:T(8,128)(2,1)S(1)} all-to-all(bf16[8,4,64,128]{3,2,1,0:T(8,128)(2,1)S(1)} %bitcast.9), channel_id=1, replica_groups=mesh['crop'=4,'y'=2,'z'=8,'x'=4,'c'=2] {'y','x'}, dimensions={0} | all-to-all | bytes 1048576 | tf_op jit(solution)/shard_map/all_to_all | solution.py:164
  53.6 0.8 %copy.7 = bf16[4,8,64,128]{3,2,1,0:T(8,128)(2,1)} copy(bf16[4,8,64,128]{3,2,0,1:T(8,128)(2,1)S(1)} %bitcast.10) | data formatting | bytes 1048576 | tf_op jit(solution)/shard_map/transpose | solution.py:165
Async XLA Ops:
  1.6 34.1 %copy-start = (bf16[1024,128]{1,0:T(8,128)(2,1)S(1)}, bf16[1024,128]{1,0:T(8,128)(2,1)}, u32[]{:S(2)}) copy-start(bf16[1024,128]{1,0:T(8,128)(2,1)} %mix_ref.1) | copy-start | bytes 786436
  29.9 7.3 %collective-permute-start = (bf16[64,32,128]{2,1,0:T(8,128)(2,1)S(1)}, bf16[64,32,128]{2,1,0:T(8,128)(2,1)S(1)}, u32[]{:S(2)}, u32[]{:S(2)}) collective-permute-start(bf16[64,32,128]{2,1,0:T(8,128)(2,1)S(1)} %all_to_all.10.own_ref), channel_id=1, source_target_pairs={{0,1},{1,0},{2,3},{3,2},{4,5},{5,4},{6,7},{7,6},{8,9},{9,8},{10,11... | collective-permute-start | bytes 1572872 | tf_op jit(solution)/shard_map/ppermute | solution.py:133

commit v4 on v3

--- a/solution.py
+++ b/solution.py
@@ -14,11 +14,12 @@
 MIB = 1024 * 1024
 
 
-def project_kernel(x_hbm, gain_hbm, first_hbm, second_hbm, message_ref, x_ref, gain_ref, first_ref, second_ref, rows_ref, sems):
+def project_kernel(x_hbm, gain_hbm, first_hbm, second_hbm, offset_hbm, message_ref, offset_ref, x_ref, gain_ref, first_ref, second_ref, rows_ref, sems):
     small = [
         pltpu.make_async_copy(gain_hbm, gain_ref, sems.at[4]),
         pltpu.make_async_copy(first_hbm, first_ref, sems.at[5]),
         pltpu.make_async_copy(second_hbm, second_ref, sems.at[6]),
+        pltpu.make_async_copy(offset_hbm, offset_ref, sems.at[7]),
     ]
     chunks = [
         pltpu.make_async_copy(x_hbm.at[pl.ds(k * 128, 128)], x_ref.at[pl.ds(k * 128, 128)], sems.at[k])
@@ -55,21 +56,22 @@
                 message_ref[(y * Z + z) * X + xx, :16, :] = block
 
 
-def spread(core, half_ref, flat_ref, lhs_ref, right_ref):
-    flat_ref[...] = half_ref[...].astype(F32).reshape(64 * 32, 128)
+def spread_left(core, flat_ref, write):
     for owner in range(8):
         block = flat_ref[pl.ds(owner * 2 + core, 64, stride=32), :]
         both = jnp.concatenate([block, pltpu.roll(block, 96, 1)], axis=0).T.astype(BF16)
-        lhs_ref[owner * 64 : owner * 64 + 32] = both[:32]
-        lhs_ref[owner * 64 + 32 : owner * 64 + 64] = both[64:96]
+        write(owner * 64, both[:32])
+        write(owner * 64 + 32, both[64:96])
+
+
+def spread_right(row, flat_ref):
     low = lax.broadcasted_iota(jnp.int32, (64, 128), 1) < 64
     zero = jnp.zeros((64, 128), F32)
-    for row in range(16):
-        block = flat_ref[pl.ds(16 + row, 64, stride=32), :]
-        rolled = pltpu.roll(block, 64, 1)
-        for e, lower, upper in ((row, block, rolled), (row + 16, rolled, block)):
-            right_ref[:64, e * 128 : e * 128 + 128] = jnp.where(low, lower, zero).astype(BF16)
-            right_ref[64:, e * 128 : e * 128 + 128] = jnp.where(low, zero, upper).astype(BF16)
+    block = flat_ref[pl.ds(16 + row, 64, stride=32), :]
+    rolled = pltpu.roll(block, 64, 1)
+    upper = jnp.concatenate([jnp.where(low, block, zero), jnp.where(low, rolled, zero)], axis=1)
+    lower = jnp.concatenate([jnp.where(low, zero, rolled), jnp.where(low, zero, block)], axis=1)
+    return jnp.concatenate([upper, lower], axis=0).astype(BF16)
 
 
 def own_kernel(core_ref, own_ref, mix_ref, lhs_ref, right_ref, mixer_ref, flat_ref, wide_ref):
@@ -77,33 +79,42 @@
     for e in range(0, 32, 4):
         rows = [wide_ref[pl.ds(e + k, 32, stride=32), :] for k in range(4)]
         mixer_ref[:, e * 32 : e * 32 + 128] = jnp.concatenate(rows, axis=0).T.astype(BF16)
-    spread(core_ref[0], own_ref, flat_ref, lhs_ref, right_ref)
+    flat_ref[...] = own_ref[...].astype(F32).reshape(64 * 32, 128)
+
+    def write(at, value):
+        lhs_ref[at : at + 32] = value
+
+    spread_left(core_ref[0], flat_ref, write)
+    for row in range(16):
+        right_ref[:, row * 256 : row * 256 + 256] = spread_right(row, flat_ref)
 
 
-def pair_kernel(core_ref, other_ref, lhs_ref, right_ref, mixer_ref, offset_hbm, out_ref, flat_ref, lhs2_ref, right2_ref, outer_ref, offset_ref, sem):
-    copy = pltpu.make_async_copy(offset_hbm, offset_ref, sem)
-    copy.start()
-    spread(core_ref[0], other_ref, flat_ref, lhs2_ref, right2_ref)
-    lhs = jnp.concatenate([lhs_ref[...], lhs2_ref[...]], axis=1)
-    for pair in range(16):
-        at = slice(pair * 256, pair * 256 + 256)
-        right = jnp.concatenate([right_ref[:, at], right2_ref[:, at]], axis=0)
-        product = jnp.dot(lhs, right, preferred_element_type=F32).astype(BF16)
+def pair_kernel(core_ref, other_ref, lhs_ref, right_ref, mixer_ref, offset_ref, out_ref, flat_ref, both_ref, outer_ref):
+    flat_ref[...] = other_ref[...].astype(F32).reshape(64 * 32, 128)
+
+    def write(at, value):
+        both_ref[at : at + 32, 128:] = value
+
+    spread_left(core_ref[0], flat_ref, write)
+    both_ref[:, :128] = lhs_ref[...]
+    for row in range(16):
+        right = jnp.concatenate(
+            [right_ref[:, row * 256 : row * 256 + 256], spread_right(row, flat_ref)], axis=0
+        )
+        product = jnp.dot(both_ref[...], right, preferred_element_type=F32).astype(BF16)
         for half in range(2):
-            e = pair * 2 + half
-            for row in range(16):
-                outer_ref[e * 32 : e * 32 + 32, row * 128 : row * 128 + 128] = product[
-                    row * 32 : row * 32 + 32, half * 128 : half * 128 + 128
+            e = row + 16 * half
+            for owner in range(16):
+                outer_ref[e * 32 : e * 32 + 32, owner * 128 : owner * 128 + 128] = product[
+                    owner * 32 : owner * 32 + 32, half * 128 : half * 128 + 128
                 ]
-    copy.wait()
-    offset = offset_ref[...]
     for pair in range(8):
         result = jnp.dot(
             mixer_ref[...], outer_ref[:, pair * 256 : pair * 256 + 256], preferred_element_type=F32
         )
         for half in range(2):
             block = result[:, half * 128 : half * 128 + 128].T
-            out_ref[pair * 2 + half] = (block * (1.0 / 128) + offset).astype(BF16)
+            out_ref[pair * 2 + half] = (block * (1.0 / 128) + offset_ref[...]).astype(BF16)
 
 
 def in_hbm(array):
@@ -114,21 +125,30 @@
     hbm = pl.BlockSpec(memory_space=pltpu.HBM)
     vmem = pl.BlockSpec(memory_space=pltpu.VMEM)
     smem = pl.BlockSpec(memory_space=pltpu.SMEM)
-    message = pl.pallas_call(
+    message, bias = pl.pallas_call(
         project_kernel,
-        out_shape=jax.ShapeDtypeStruct((64, 32, 128), BF16),
-        in_specs=[hbm] * 4,
-        out_specs=vmem,
+        out_shape=(
+            jax.ShapeDtypeStruct((64, 32, 128), BF16),
+            jax.ShapeDtypeStruct((1, 128), F32),
+        ),
+        in_specs=[hbm] * 5,
+        out_specs=(vmem, vmem),
         scratch_shapes=[
             pltpu.VMEM((512, 256), BF16),
             pltpu.VMEM((1, 256), F32),
             pltpu.VMEM((32, 256), BF16),
             pltpu.VMEM((32, 256), BF16),
             pltpu.VMEM((512, 128), F32),
-            pltpu.SemaphoreType.DMA((7,)),
+            pltpu.SemaphoreType.DMA((8,)),
         ],
         compiler_params=pltpu.CompilerParams(vmem_limit_bytes=32 * MIB),
-    )(in_hbm(x.reshape(512, 256)), in_hbm(gain.reshape(1, 256)), in_hbm(first.T), in_hbm(second.T))
+    )(
+        in_hbm(x.reshape(512, 256)),
+        in_hbm(gain.reshape(1, 256)),
+        in_hbm(first.T),
+        in_hbm(second.T),
+        in_hbm(offset.reshape(1, 128)),
+    )
     own = lax.all_to_all(message, CHIP, split_axis=0, concat_axis=0, tiled=True)
     other = lax.ppermute(own, "c", [(0, 1), (1, 0)])
     core = lax.axis_index("c").reshape(1)
@@ -148,18 +168,15 @@
     tile = pl.pallas_call(
         pair_kernel,
         out_shape=jax.ShapeDtypeStruct((16, 128, 128), BF16),
-        in_specs=[smem, vmem, vmem, vmem, vmem, hbm],
+        in_specs=[smem] + [vmem] * 5,
         out_specs=vmem,
         scratch_shapes=[
             pltpu.VMEM((64 * 32, 128), F32),
-            pltpu.VMEM((512, 128), BF16),
-            pltpu.VMEM((128, 4096), BF16),
+            pltpu.VMEM((512, 256), BF16),
             pltpu.VMEM((1024, 2048), BF16),
-            pltpu.VMEM((1, 128), F32),
-            pltpu.SemaphoreType.DMA,
         ],
         compiler_params=pltpu.CompilerParams(vmem_limit_bytes=32 * MIB),
-    )(core, other, lhs, right, mixer, in_hbm(offset.reshape(1, 128)))
+    )(core, other, lhs, right, mixer, bias)
     tile = tile.reshape(8, 4, 64, 128)
     got = lax.all_to_all(tile, COLUMN, split_axis=0, concat_axis=0, tiled=True)
     return got.transpose(1, 0, 2, 3).reshape(4, 512, 128)

time: 55.3 us -> 54.6 us (0.987)
  Pallas kernels: 6.04 us -> 5.34 us
    pallas_call x1, Pallas kernels: 3.28 us -> 2.55 us  [body(): pl.pallas_call(pair_kernel, out_shape=jax.ShapeDtypeStruct((16, 128, 128)...]
where the time goes in v4:
time: 54.6 us; the launch traced here: 53.7 us
  blocking collectives  41.3 us (76%)
  starting transfers between devices  5.81 us (11%)
  Pallas kernels  5.34 us (10%)
  local copies, waits for them, and re-layouts  0.84 us (2%)
    all_to_all x1, blocking collectives, body(): own = lax.all_to_all(message, CHIP, split_axis=0, concat_axis=0, tiled=True)  28.3 us
    all_to_all x1, blocking collectives, body(): got = lax.all_to_all(tile, COLUMN, split_axis=0, concat_axis=0, tiled=True)  13 us
    ppermute x1, starting transfers between devices, body(): other = lax.ppermute(own, 'c', [(0, 1), (1, 0)])  5.81 us
    pallas_call x1, Pallas kernels, body(): pl.pallas_call(pair_kernel, out_shape=jax.ShapeDtypeStruct((16, 128, 128)...  2.55 us
    pallas_call x1, Pallas kernels, body(): pl.pallas_call(project_kernel, out_shape=(jax.ShapeDtypeStruct((64, 32, 1...  1.6 us
    pallas_call x1, Pallas kernels, body(): pl.pallas_call(own_kernel, out_shape=(jax.ShapeDtypeStruct((512, 128), BF...  1.2 us
  transfers between devices with their start and end apart: 1, of which 1 were waited for; matrix products, arithmetic and copies ran while one was open for 0% of the time, Pallas kernels for 2%

profile of v4, /device:TPU:1, one launch (start us, length us, event | category | flops | bytes accessed | tf_op | source)
XLA Modules:
  0.0 53.7 jit_solution(18027817844934097562)
XLA Ops:
  0.0 1.6 %shard_map.64 = (bf16[64,32,128]{2,1,0:T(8,128)(2,1)S(1)}, f32[1,128]{1,0:T(1,128)S(1)}) custom-call(bf16[512,256]{1,0:T(8,128)(2,1)} %bitcast.11, f32[1,256]{1,0:T(1,128)} %bitcast.14, bf16[32,256]{1,0:T(8,128)(2,1)} %bitcast.12, bf16[32,256]{1,0:T(8,128)(2,1)} %bitcast.13, f32[1,128]{1,0:T(1,128)} %bitcast.15), custom_call_target="tpu_custom_call" | custom-call | tf_op jit(solution)/shard_map/pallas_call | solution.py:128
  1.6 0.0 copy-start
  1.6 28.3 %all_to_all.10.own_ref = bf16[64,32,128]{2,1,0:T(8,128)(2,1)S(1)} all-to-all(bf16[64,32,128]{2,1,0:T(8,128)(2,1)S(1)} %get-tuple-element.10), channel_id=1, replica_groups=mesh['crop'=4,'y'=2,'z'=8,'x'=4,'c'=2] {'y','z','x'}, dimensions={0} | all-to-all | bytes 1048576 | tf_op jit(solution)/shard_map/all_to_all | solution.py:152
  29.9 5.8 %collective-permute-start = (bf16[64,32,128]{2,1,0:T(8,128)(2,1)S(1)}, bf16[64,32,128]{2,1,0:T(8,128)(2,1)S(1)}, u32[]{:S(2)}, u32[]{:S(2)}) collective-permute-start(bf16[64,32,128]{2,1,0:T(8,128)(2,1)S(1)} %all_to_all.10.own_ref), channel_id=1, source_target_pairs={{0,1},{1,0},{2,3},{3,2},{4,5},{5,4},{6,7},{7,6},{8,9},{9,8},{10,11... | collective-permute-start | bytes 1572872 | tf_op jit(solution)/shard_map/ppermute | solution.py:153
  35.8 0.0 copy-done
  35.8 1.2 %shard_map.65 = (bf16[512,128]{1,0:T(8,128)(2,1)S(1)}, bf16[128,4096]{1,0:T(8,128)(2,1)S(1)}, bf16[128,1024]{1,0:T(8,128)(2,1)S(1)}) custom-call(s32[1]{0:T(128)} %bitcast.core_ref, bf16[64,32,128]{2,1,0:T(8,128)(2,1)S(1)} %all_to_all.10.own_ref, bf16[1024,128]{1,0:T(8,128)(2,1)S(1)} %copy-done), custom_call_target="tpu_custom_call" | custom-call | flops 2000000 | bytes 2000000 | tf_op jit(solution)/shard_map/pallas_call | solution.py:155
  37.0 0.3 collective-permute-done.other_ref
  37.3 2.5 %shard_map.66 = bf16[16,128,128]{2,1,0:T(8,128)(2,1)S(1)} custom-call(s32[1]{0:T(128)} %bitcast.core_ref, bf16[64,32,128]{2,1,0:T(8,128)(2,1)S(1)} %collective-permute-done.other_ref, bf16[512,128]{1,0:T(8,128)(2,1)S(1)} %get-tuple-element.11.lhs_ref, bf16[128,4096]{1,0:T(8,128)(2,1)S(1)} %get-tuple-element.12.right_ref, ...), custom_call_target="tpu_custom_call" | custom-call | tf_op jit(solution)/shard_map/pallas_call | solution.py:168
  39.8 13.0 %all_to_all.11 = bf16[8,4,64,128]{3,2,1,0:T(8,128)(2,1)S(1)} all-to-all(bf16[8,4,64,128]{3,2,1,0:T(8,128)(2,1)S(1)} %bitcast.9), channel_id=1, replica_groups=mesh['crop'=4,'y'=2,'z'=8,'x'=4,'c'=2] {'y','x'}, dimensions={0} | all-to-all | bytes 1048576 | tf_op jit(solution)/shard_map/all_to_all | solution.py:181
  52.9 0.8 %copy.7 = bf16[4,8,64,128]{3,2,1,0:T(8,128)(2,1)} copy(bf16[4,8,64,128]{3,2,0,1:T(8,128)(2,1)S(1)} %bitcast.10) | data formatting | bytes 1048576 | tf_op jit(solution)/shard_map/transpose | solution.py:182
Async XLA Ops:
  1.6 34.1 %copy-start = (bf16[1024,128]{1,0:T(8,128)(2,1)S(1)}, bf16[1024,128]{1,0:T(8,128)(2,1)}, u32[]{:S(2)}) copy-start(bf16[1024,128]{1,0:T(8,128)(2,1)} %mix_ref.1) | copy-start | bytes 786436
  29.9 7.3 %collective-permute-start = (bf16[64,32,128]{2,1,0:T(8,128)(2,1)S(1)}, bf16[64,32,128]{2,1,0:T(8,128)(2,1)S(1)}, u32[]{:S(2)}, u32[]{:S(2)}) collective-permute-start(bf16[64,32,128]{2,1,0:T(8,128)(2,1)S(1)} %all_to_all.10.own_ref), channel_id=1, source_target_pairs={{0,1},{1,0},{2,3},{3,2},{4,5},{5,4},{6,7},{7,6},{8,9},{9,8},{10,11... | collective-permute-start | bytes 1572872 | tf_op jit(solution)/shard_map/ppermute | solution.py:153

commit v5 on v4

--- a/solution.py
+++ b/solution.py
@@ -64,43 +64,42 @@
         write(owner * 64 + 32, both[64:96])
 
 
-def spread_right(row, flat_ref):
+def spread_right(block):
     low = lax.broadcasted_iota(jnp.int32, (64, 128), 1) < 64
     zero = jnp.zeros((64, 128), F32)
-    block = flat_ref[pl.ds(16 + row, 64, stride=32), :]
+    block = block.astype(F32)
     rolled = pltpu.roll(block, 64, 1)
     upper = jnp.concatenate([jnp.where(low, block, zero), jnp.where(low, rolled, zero)], axis=1)
     lower = jnp.concatenate([jnp.where(low, zero, rolled), jnp.where(low, zero, block)], axis=1)
     return jnp.concatenate([upper, lower], axis=0).astype(BF16)
 
 
-def own_kernel(core_ref, own_ref, mix_ref, lhs_ref, right_ref, mixer_ref, flat_ref, wide_ref):
+def share_kernel(core_ref, own_ref, mix_ref, lhs_ref, share_ref, mixer_ref, flat_ref, wide_ref):
+    flat_ref[...] = own_ref[...].astype(F32).reshape(64 * 32, 128)
+
+    def write_own(at, value):
+        lhs_ref[at : at + 32] = value
+
+    def write_other(at, value):
+        share_ref[at : at + 32] = value
+
+    spread_left(core_ref[0], flat_ref, write_own)
+    spread_left(1 - core_ref[0], flat_ref, write_other)
+    for row in range(16):
+        share_ref[512 + row * 64 : 576 + row * 64] = flat_ref[pl.ds(16 + row, 64, stride=32), :].astype(BF16)
     wide_ref[...] = mix_ref[...].astype(F32)
     for e in range(0, 32, 4):
         rows = [wide_ref[pl.ds(e + k, 32, stride=32), :] for k in range(4)]
         mixer_ref[:, e * 32 : e * 32 + 128] = jnp.concatenate(rows, axis=0).T.astype(BF16)
-    flat_ref[...] = own_ref[...].astype(F32).reshape(64 * 32, 128)
-
-    def write(at, value):
-        lhs_ref[at : at + 32] = value
-
-    spread_left(core_ref[0], flat_ref, write)
-    for row in range(16):
-        right_ref[:, row * 256 : row * 256 + 256] = spread_right(row, flat_ref)
 
 
-def pair_kernel(core_ref, other_ref, lhs_ref, right_ref, mixer_ref, offset_ref, out_ref, flat_ref, both_ref, outer_ref):
-    flat_ref[...] = other_ref[...].astype(F32).reshape(64 * 32, 128)
-
-    def write(at, value):
-        both_ref[at : at + 32, 128:] = value
-
-    spread_left(core_ref[0], flat_ref, write)
+def pair_kernel(core_ref, shares_ref, lhs_ref, share_ref, mixer_ref, offset_ref, out_ref, both_ref, outer_ref):
+    other = 1 - core_ref[0]
     both_ref[:, :128] = lhs_ref[...]
+    both_ref[:, 128:] = shares_ref[other, :512]
     for row in range(16):
-        right = jnp.concatenate(
-            [right_ref[:, row * 256 : row * 256 + 256], spread_right(row, flat_ref)], axis=0
-        )
+        at = slice(512 + row * 64, 576 + row * 64)
+        right = jnp.concatenate([spread_right(share_ref[at]), spread_right(shares_ref[other, at])], axis=0)
         product = jnp.dot(both_ref[...], right, preferred_element_type=F32).astype(BF16)
         for half in range(2):
             e = row + 16 * half
@@ -149,34 +148,32 @@
         in_hbm(second.T),
         in_hbm(offset.reshape(1, 128)),
     )
+    message, core = lax.optimization_barrier((message, lax.axis_index("c").reshape(1)))
     own = lax.all_to_all(message, CHIP, split_axis=0, concat_axis=0, tiled=True)
-    other = lax.ppermute(own, "c", [(0, 1), (1, 0)])
-    core = lax.axis_index("c").reshape(1)
-    lhs, right, mixer = pl.pallas_call(
-        own_kernel,
+    lhs, share, mixer = pl.pallas_call(
+        share_kernel,
         out_shape=(
             jax.ShapeDtypeStruct((512, 128), BF16),
-            jax.ShapeDtypeStruct((128, 4096), BF16),
+            jax.ShapeDtypeStruct((1536, 128), BF16),
             jax.ShapeDtypeStruct((128, 1024), BF16),
         ),
         in_specs=[smem, vmem, vmem],
         out_specs=(vmem, vmem, vmem),
         scratch_shapes=[pltpu.VMEM((64 * 32, 128), F32), pltpu.VMEM((1024, 128), F32)],
         compiler_params=pltpu.CompilerParams(vmem_limit_bytes=32 * MIB),
-        cost_estimate=pl.CostEstimate(flops=2_000_000, bytes_accessed=2_000_000, transcendentals=0),
     )(core, own, mix)
+    shares = lax.all_gather(share, "c", axis=0, tiled=False)
     tile = pl.pallas_call(
         pair_kernel,
         out_shape=jax.ShapeDtypeStruct((16, 128, 128), BF16),
         in_specs=[smem] + [vmem] * 5,
         out_specs=vmem,
         scratch_shapes=[
-            pltpu.VMEM((64 * 32, 128), F32),
             pltpu.VMEM((512, 256), BF16),
             pltpu.VMEM((1024, 2048), BF16),
         ],
         compiler_params=pltpu.CompilerParams(vmem_limit_bytes=32 * MIB),
-    )(core, other, lhs, right, mixer, bias)
+    )(core, shares, lhs, share, mixer, bias)
     tile = tile.reshape(8, 4, 64, 128)
     got = lax.all_to_all(tile, COLUMN, split_axis=0, concat_axis=0, tiled=True)
     return got.transpose(1, 0, 2, 3).reshape(4, 512, 128)

time: 54.6 us -> 54 us (0.989)
  blocking collectives: 41.3 us -> 47.3 us
  starting transfers between devices: 5.81 us -> 0 us
    all_gather x0 -> x1, blocking collectives: none -> 5.91 us  [body(): shares = lax.all_gather(share, 'c', axis=0, tiled=False)]
    ppermute x1 -> x0, starting transfers between devices: 5.81 us -> none  [body(): other = lax.ppermute(own, 'c', [(0, 1), (1, 0)])]
  transfers between devices with their start and end apart: 1 -> 0, of which waited for: 1 -> 0; matrix products, arithmetic and copies ran while one was open for 0% -> 0% of each run, Pallas kernels for 2% -> 0%
where the time goes in v5:
time: 54 us; the launch traced here: 53.1 us
  blocking collectives  47.3 us (88%)
  Pallas kernels  4.97 us (9%)
  local copies, waits for them, and re-layouts  0.84 us (2%)
    all_to_all x1, blocking collectives, body(): own = lax.all_to_all(message, CHIP, split_axis=0, concat_axis=0, tiled=True)  28.3 us
    all_to_all x1, blocking collectives, body(): got = lax.all_to_all(tile, COLUMN, split_axis=0, concat_axis=0, tiled=True)  13 us
    all_gather x1, blocking collectives, body(): shares = lax.all_gather(share, 'c', axis=0, tiled=False)  5.91 us
    pallas_call x1, Pallas kernels, body(): pl.pallas_call(pair_kernel, out_shape=jax.ShapeDtypeStruct((16, 128, 128)...  2.03 us
    pallas_call x1, Pallas kernels, body(): pl.pallas_call(project_kernel, out_shape=(jax.ShapeDtypeStruct((64, 32, 1...  1.6 us
    pallas_call x1, Pallas kernels, body(): pl.pallas_call(share_kernel, out_shape=(jax.ShapeDtypeStruct((512, 128),...  1.34 us

profile of v5, /device:TPU:1, one launch (start us, length us, event | category | flops | bytes accessed | tf_op | source)
XLA Modules:
  0.0 53.1 jit_solution(7601244451364322438)
XLA Ops:
  0.0 1.6 %shard_map.64 = (bf16[64,32,128]{2,1,0:T(8,128)(2,1)S(1)}, f32[1,128]{1,0:T(1,128)S(1)}) custom-call(bf16[512,256]{1,0:T(8,128)(2,1)} %bitcast.13, f32[1,256]{1,0:T(1,128)} %bitcast.16, bf16[32,256]{1,0:T(8,128)(2,1)} %bitcast.14, bf16[32,256]{1,0:T(8,128)(2,1)} %bitcast.15, f32[1,128]{1,0:T(1,128)} %bitcast.17), custom_call_target="tpu_custom_call" | custom-call | tf_op jit(solution)/shard_map/pallas_call | solution.py:127
  1.6 0.0 copy-start
  1.6 28.3 %all_to_all.10.own_ref = bf16[64,32,128]{2,1,0:T(8,128)(2,1)S(1)} all-to-all(bf16[64,32,128]{2,1,0:T(8,128)(2,1)S(1)} %get-tuple-element.14), channel_id=1, replica_groups=mesh['crop'=4,'y'=2,'z'=8,'x'=4,'c'=2] {'y','z','x'}, dimensions={0} | all-to-all | bytes 1048576 | tf_op jit(solution)/shard_map/all_to_all | solution.py:152
  29.9 0.0 copy-done
  29.9 1.3 %shard_map.65 = (bf16[512,128]{1,0:T(8,128)(2,1)S(1)}, bf16[1536,128]{1,0:T(8,128)(2,1)S(1)}, bf16[128,1024]{1,0:T(8,128)(2,1)S(1)}) custom-call(s32[1]{0:T(128)} %bitcast.5.core_ref, bf16[64,32,128]{2,1,0:T(8,128)(2,1)S(1)} %all_to_all.10.own_ref, bf16[1024,128]{1,0:T(8,128)(2,1)S(1)} %copy-done), custom_call_target="tpu_custom_call" | custom-call | tf_op jit(solution)/shard_map/pallas_call | solution.py:153
  31.3 5.9 %all-gather = bf16[3072,128]{1,0:T(8,128)(2,1)S(1)} all-gather(bf16[1536,128]{1,0:T(8,128)(2,1)S(1)} %get-tuple-element.15.share_ref), channel_id=2, replica_groups=mesh['crop'=4,'y'=2,'z'=8,'x'=4,'c'=2] {'c'}, dimensions={0}, use_global_device_ids=true | all-gather | bytes 1179648 | tf_op jit(solution)/shard_map/all_gather | solution.py:165
  37.2 2.0 %shard_map.66 = bf16[16,128,128]{2,1,0:T(8,128)(2,1)S(1)} custom-call(s32[1]{0:T(128)} %bitcast.5.core_ref, bf16[2,1536,128]{2,1,0:T(8,128)(2,1)S(1)} %bitcast.10, bf16[512,128]{1,0:T(8,128)(2,1)S(1)} %get-tuple-element.16.lhs_ref, bf16[1536,128]{1,0:T(8,128)(2,1)S(1)} %get-tuple-element.15.share_ref, bf16[128,1024]{1,0:T(8,128)(2,1)S(1)} %get-tuple-element.17.mixer_ref, ...), custom_call_target="tpu_custom_call" | custom-call | tf_op jit(solution)/shard_map/pallas_call | solution.py:166
  39.2 13.0 %all_to_all.11 = bf16[8,4,64,128]{3,2,1,0:T(8,128)(2,1)S(1)} all-to-all(bf16[8,4,64,128]{3,2,1,0:T(8,128)(2,1)S(1)} %bitcast.11), channel_id=1, replica_groups=mesh['crop'=4,'y'=2,'z'=8,'x'=4,'c'=2] {'y','x'}, dimensions={0} | all-to-all | bytes 1048576 | tf_op jit(solution)/shard_map/all_to_all | solution.py:178
  52.3 0.8 %copy.7 = bf16[4,8,64,128]{3,2,1,0:T(8,128)(2,1)} copy(bf16[4,8,64,128]{3,2,0,1:T(8,128)(2,1)S(1)} %bitcast.12) | data formatting | bytes 1048576 | tf_op jit(solution)/shard_map/transpose | solution.py:179
Async XLA Ops:
  1.6 28.3 %copy-start = (bf16[1024,128]{1,0:T(8,128)(2,1)S(1)}, bf16[1024,128]{1,0:T(8,128)(2,1)}, u32[]{:S(2)}) copy-start(bf16[1024,128]{1,0:T(8,128)(2,1)} %mix_ref.1) | copy-start | bytes 786436

commit v6 on v5

--- a/solution.py
+++ b/solution.py
@@ -3,13 +3,15 @@
 from jax import lax
 from jax.experimental import pallas as pl
 from jax.experimental.pallas import tpu as pltpu
-from jax.sharding import Mesh, PartitionSpec as P
+from jax.sharding import PartitionSpec as P
 
 Y, Z, X, C = 2, 8, 4, 2
 F32, BF16 = jnp.float32, jnp.bfloat16
-CHIP = ("y", "z", "x")
-COLUMN = ("y", "x")
-ALL = ("crop", "y", "z", "x", "c")
+ORDER = [(y, z, x) for y in range(Y) for z in reversed(range(Z)) for x in range(X)]
+PLACE = [[[ORDER.index((y, z, x)) for x in range(X)] for z in range(Z)] for y in range(Y)]
+CHIP = [[((y * Z + z) * X + x) * C + c for y, z, x in ORDER] for c in range(C)]
+COLUMN = [[((y * Z + z) * X + x) * C + c for y in range(Y) for x in range(X)] for z in range(Z) for c in range(C)]
+PAIR = [[2 * k, 2 * k + 1] for k in range(Y * Z * X)]
 NT = (((1,), (1,)), ((), ()))
 MIB = 1024 * 1024
 
@@ -44,7 +46,7 @@
         odd = jnp.where(low, pltpu.roll(head, 64, 1), tail).astype(BF16)
         for which, block in ((2 * k, even), (2 * k + 1, odd)):
             for z in range(Z):
-                message_ref[(which // X * Z + z) * X + which % X, 16:, :] = block
+                message_ref[PLACE[which // X][z][which % X], 16:, :] = block
     group = lax.broadcasted_iota(jnp.int32, (128, 128), 1) // 32
     left = rows_ref[pl.ds(0, 128, stride=4), :]
     for r in range(1, 4):
@@ -53,7 +55,7 @@
         block = jnp.concatenate([left[z * 8 : z * 8 + 8], left[64 + z * 8 : 72 + z * 8]], axis=0).astype(BF16)
         for y in range(Y):
             for xx in range(X):
-                message_ref[(y * Z + z) * X + xx, :16, :] = block
+                message_ref[PLACE[y][z][xx], :16, :] = block
 
 
 def spread_left(core, flat_ref, write):
@@ -148,8 +150,8 @@
         in_hbm(second.T),
         in_hbm(offset.reshape(1, 128)),
     )
-    message, core = lax.optimization_barrier((message, lax.axis_index("c").reshape(1)))
-    own = lax.all_to_all(message, CHIP, split_axis=0, concat_axis=0, tiled=True)
+    message, core = lax.optimization_barrier((message, (lax.axis_index("res") % C).reshape(1)))
+    own = lax.all_to_all(message, "res", split_axis=0, concat_axis=0, tiled=True, axis_index_groups=CHIP)
     lhs, share, mixer = pl.pallas_call(
         share_kernel,
         out_shape=(
@@ -162,7 +164,7 @@
         scratch_shapes=[pltpu.VMEM((64 * 32, 128), F32), pltpu.VMEM((1024, 128), F32)],
         compiler_params=pltpu.CompilerParams(vmem_limit_bytes=32 * MIB),
     )(core, own, mix)
-    shares = lax.all_gather(share, "c", axis=0, tiled=False)
+    shares = lax.all_gather(share, "res", axis=0, tiled=False, axis_index_groups=PAIR)
     tile = pl.pallas_call(
         pair_kernel,
         out_shape=jax.ShapeDtypeStruct((16, 128, 128), BF16),
@@ -175,13 +177,12 @@
         compiler_params=pltpu.CompilerParams(vmem_limit_bytes=32 * MIB),
     )(core, shares, lhs, share, mixer, bias)
     tile = tile.reshape(8, 4, 64, 128)
-    got = lax.all_to_all(tile, COLUMN, split_axis=0, concat_axis=0, tiled=True)
+    got = lax.all_to_all(tile, "res", split_axis=0, concat_axis=0, tiled=True, axis_index_groups=COLUMN)
     return got.transpose(1, 0, 2, 3).reshape(4, 512, 128)
 
 
 def solution(mesh):
-    fine = Mesh(mesh.devices.reshape(mesh.devices.shape[0], Y, Z, X, C), ALL)
-    split = P(ALL, None, None)
+    split = P(("crop", "res"), None, None)
     return jax.shard_map(
-        body, mesh=fine, in_specs=(split, P(), P(), P(), P(), P()), out_specs=split, check_vma=False
+        body, mesh=mesh, in_specs=(split, P(), P(), P(), P(), P()), out_specs=split, check_vma=False
     )

time: 54 us -> 52.3 us (0.969)
  blocking collectives: 47.3 us -> 45.6 us
    all_to_all x2, blocking collectives: 41.3 us -> 38.1 us  [the longest x1 26 us: body(): lax.all_to_all(message, 'res', split_axis=0, concat_axis=0, tiled=True, a...]
    all_gather x1, blocking collectives: 5.91 us -> 7.48 us  [body(): lax.all_gather(share, 'res', axis=0, tiled=False, axis_index_groups=PAIR)]
where the time goes in v6:
time: 52.3 us; the launch traced here: 51.5 us
  blocking collectives  45.6 us (87%)
  Pallas kernels  4.97 us (10%)
  local copies, waits for them, and re-layouts  0.84 us (2%)
    all_to_all x1, blocking collectives, body(): lax.all_to_all(message, 'res', split_axis=0, concat_axis=0, tiled=True, a...  26 us
    all_to_all x1, blocking collectives, body(): lax.all_to_all(tile, 'res', split_axis=0, concat_axis=0, tiled=True, axis...  12.1 us
    all_gather x1, blocking collectives, body(): lax.all_gather(share, 'res', axis=0, tiled=False, axis_index_groups=PAIR)  7.48 us
    pallas_call x1, Pallas kernels, body(): pl.pallas_call(pair_kernel, out_shape=jax.ShapeDtypeStruct((16, 128, 128)...  2.02 us
    pallas_call x1, Pallas kernels, body(): pl.pallas_call(project_kernel, out_shape=(jax.ShapeDtypeStruct((64, 32, 1...  1.6 us
    pallas_call x1, Pallas kernels, body(): pl.pallas_call(share_kernel, out_shape=(jax.ShapeDtypeStruct((512, 128),...  1.34 us

profile of v6, /device:TPU:1, one launch (start us, length us, event | category | flops | bytes accessed | tf_op | source)
XLA Modules:
  0.0 51.5 jit_solution(9813062632031271570)
XLA Ops:
  0.0 1.6 %shard_map.64 = (bf16[64,32,128]{2,1,0:T(8,128)(2,1)S(1)}, f32[1,128]{1,0:T(1,128)S(1)}) custom-call(bf16[512,256]{1,0:T(8,128)(2,1)} %bitcast.13, f32[1,256]{1,0:T(1,128)} %bitcast.16, bf16[32,256]{1,0:T(8,128)(2,1)} %bitcast.14, bf16[32,256]{1,0:T(8,128)(2,1)} %bitcast.15, f32[1,128]{1,0:T(1,128)} %bitcast.17), custom_call_target="tpu_custom_call" | custom-call | tf_op jit(solution)/shard_map/pallas_call | solution.py:129
  1.6 0.0 copy-start
  1.6 26.0 %all_to_all.10.own_ref = bf16[64,32,128]{2,1,0:T(8,128)(2,1)S(1)} all-to-all(bf16[64,32,128]{2,1,0:T(8,128)(2,1)S(1)} %get-tuple-element.14), channel_id=1, replica_groups={{56,58,60,62,48,50,52,54,40,42,44,46,32,34,36,38,24,26,28,30,16,18,20,2..., dimensions={0} | all-to-all | bytes 1048576 | tf_op jit(solution)/shard_map/all_to_all | solution.py:154
  27.6 0.0 copy-done
  27.6 1.3 %shard_map.65 = (bf16[512,128]{1,0:T(8,128)(2,1)S(1)}, bf16[1536,128]{1,0:T(8,128)(2,1)S(1)}, bf16[128,1024]{1,0:T(8,128)(2,1)S(1)}) custom-call(s32[1]{0:T(128)} %bitcast.5.core_ref, bf16[64,32,128]{2,1,0:T(8,128)(2,1)S(1)} %all_to_all.10.own_ref, bf16[1024,128]{1,0:T(8,128)(2,1)S(1)} %copy-done), custom_call_target="tpu_custom_call" | custom-call | tf_op jit(solution)/shard_map/pallas_call | solution.py:155
  29.0 7.5 %all-gather = bf16[3072,128]{1,0:T(8,128)(2,1)S(1)} all-gather(bf16[1536,128]{1,0:T(8,128)(2,1)S(1)} %get-tuple-element.15.share_ref), channel_id=2, replica_groups={{0,1},{2,3},{4,5},{6,7},{8,9},{10,11},{12,13},{14,15},{16,17},{18,19},{..., dimensions={0}, use_global_device_ids=true | all-gather | bytes 1179648 | tf_op jit(solution)/shard_map/all_gather | solution.py:167
  36.5 2.0 %shard_map.66 = bf16[16,128,128]{2,1,0:T(8,128)(2,1)S(1)} custom-call(s32[1]{0:T(128)} %bitcast.5.core_ref, bf16[2,1536,128]{2,1,0:T(8,128)(2,1)S(1)} %bitcast.10, bf16[512,128]{1,0:T(8,128)(2,1)S(1)} %get-tuple-element.16.lhs_ref, bf16[1536,128]{1,0:T(8,128)(2,1)S(1)} %get-tuple-element.15.share_ref, bf16[128,1024]{1,0:T(8,128)(2,1)S(1)} %get-tuple-element.17.mixer_ref, ...), custom_call_target="tpu_custom_call" | custom-call | tf_op jit(solution)/shard_map/pallas_call | solution.py:168
  38.5 12.1 %all_to_all.11 = bf16[8,4,64,128]{3,2,1,0:T(8,128)(2,1)S(1)} all-to-all(bf16[8,4,64,128]{3,2,1,0:T(8,128)(2,1)S(1)} %bitcast.11), channel_id=1, replica_groups={{0,2,4,6,64,66,68,70},{1,3,5,7,65,67,69,71},{8,10,12,14,72,74,76,78},{9..., dimensions={0} | all-to-all | bytes 1048576 | tf_op jit(solution)/shard_map/all_to_all | solution.py:180
  50.6 0.8 %copy.7 = bf16[4,8,64,128]{3,2,1,0:T(8,128)(2,1)} copy(bf16[4,8,64,128]{3,2,0,1:T(8,128)(2,1)S(1)} %bitcast.12) | data formatting | bytes 1048576 | tf_op jit(solution)/shard_map/transpose | solution.py:181
Async XLA Ops:
  1.6 26.0 %copy-start = (bf16[1024,128]{1,0:T(8,128)(2,1)S(1)}, bf16[1024,128]{1,0:T(8,128)(2,1)}, u32[]{:S(2)}) copy-start(bf16[1024,128]{1,0:T(8,128)(2,1)} %mix_ref.1) | copy-start | bytes 786436

commit v7 on v6

--- a/solution.py
+++ b/solution.py
@@ -7,7 +7,7 @@
 
 Y, Z, X, C = 2, 8, 4, 2
 F32, BF16 = jnp.float32, jnp.bfloat16
-ORDER = [(y, z, x) for y in range(Y) for z in reversed(range(Z)) for x in range(X)]
+ORDER = [(y, z, x) for y in reversed(range(Y)) for z in reversed(range(Z)) for x in range(X)]
 PLACE = [[[ORDER.index((y, z, x)) for x in range(X)] for z in range(Z)] for y in range(Y)]
 CHIP = [[((y * Z + z) * X + x) * C + c for y, z, x in ORDER] for c in range(C)]
 COLUMN = [[((y * Z + z) * X + x) * C + c for y in range(Y) for x in range(X)] for z in range(Z) for c in range(C)]

time: 52.3 us -> 51.8 us (level)
    all_to_all x1, blocking collectives: 26 us -> 30.1 us  [body(): lax.all_to_all(message, 'res', split_axis=0, concat_axis=0, tiled=True, a...]
    all_gather x1, blocking collectives: 7.48 us -> 3.71 us  [body(): lax.all_gather(share, 'res', axis=0, tiled=False, axis_index_groups=PAIR)]
    all_to_all x1, blocking collectives: 12.1 us -> 11.2 us  [body(): lax.all_to_all(tile, 'res', split_axis=0, concat_axis=0, tiled=True, axis...]
where the time goes in v7:
time: 51.8 us; the launch traced here: 50.9 us
  blocking collectives  45.1 us (87%)
  Pallas kernels  4.96 us (10%)
  local copies, waits for them, and re-layouts  0.84 us (2%)
    all_to_all x1, blocking collectives, body(): lax.all_to_all(message, 'res', split_axis=0, concat_axis=0, tiled=True, a...  30.1 us
    all_to_all x1, blocking collectives, body(): lax.all_to_all(tile, 'res', split_axis=0, concat_axis=0, tiled=True, axis...  11.2 us
    all_gather x1, blocking collectives, body(): lax.all_gather(share, 'res', axis=0, tiled=False, axis_index_groups=PAIR)  3.71 us
    pallas_call x1, Pallas kernels, body(): pl.pallas_call(pair_kernel, out_shape=jax.ShapeDtypeStruct((16, 128, 128)...  2.02 us
    pallas_call x1, Pallas kernels, body(): pl.pallas_call(project_kernel, out_shape=(jax.ShapeDtypeStruct((64, 32, 1...  1.6 us
    pallas_call x1, Pallas kernels, body(): pl.pallas_call(share_kernel, out_shape=(jax.ShapeDtypeStruct((512, 128),...  1.34 us

profile of v7, /device:TPU:1, one launch (start us, length us, event | category | flops | bytes accessed | tf_op | source)
XLA Modules:
  0.0 50.9 jit_solution(12511775028576591681)
XLA Ops:
  0.0 1.6 %shard_map.64 = (bf16[64,32,128]{2,1,0:T(8,128)(2,1)S(1)}, f32[1,128]{1,0:T(1,128)S(1)}) custom-call(bf16[512,256]{1,0:T(8,128)(2,1)} %bitcast.13, f32[1,256]{1,0:T(1,128)} %bitcast.16, bf16[32,256]{1,0:T(8,128)(2,1)} %bitcast.14, bf16[32,256]{1,0:T(8,128)(2,1)} %bitcast.15, f32[1,128]{1,0:T(1,128)} %bitcast.17), custom_call_target="tpu_custom_call" | custom-call | tf_op jit(solution)/shard_map/pallas_call | solution.py:129
  1.6 0.0 copy-start
  1.6 30.1 %all_to_all.10.own_ref = bf16[64,32,128]{2,1,0:T(8,128)(2,1)S(1)} all-to-all(bf16[64,32,128]{2,1,0:T(8,128)(2,1)S(1)} %get-tuple-element.14), channel_id=1, replica_groups={{120,122,124,126,112,114,116,118,104,106,108,110,96,98,100,102,88,90,92..., dimensions={0} | all-to-all | bytes 1048576 | tf_op jit(solution)/shard_map/all_to_all | solution.py:154
  31.7 0.0 copy-done
  31.7 1.3 %shard_map.65 = (bf16[512,128]{1,0:T(8,128)(2,1)S(1)}, bf16[1536,128]{1,0:T(8,128)(2,1)S(1)}, bf16[128,1024]{1,0:T(8,128)(2,1)S(1)}) custom-call(s32[1]{0:T(128)} %bitcast.5.core_ref, bf16[64,32,128]{2,1,0:T(8,128)(2,1)S(1)} %all_to_all.10.own_ref, bf16[1024,128]{1,0:T(8,128)(2,1)S(1)} %copy-done), custom_call_target="tpu_custom_call" | custom-call | tf_op jit(solution)/shard_map/pallas_call | solution.py:155
  33.1 3.7 %all-gather = bf16[3072,128]{1,0:T(8,128)(2,1)S(1)} all-gather(bf16[1536,128]{1,0:T(8,128)(2,1)S(1)} %get-tuple-element.15.share_ref), channel_id=2, replica_groups={{0,1},{2,3},{4,5},{6,7},{8,9},{10,11},{12,13},{14,15},{16,17},{18,19},{..., dimensions={0}, use_global_device_ids=true | all-gather | bytes 1179648 | tf_op jit(solution)/shard_map/all_gather | solution.py:167
  36.8 2.0 %shard_map.66 = bf16[16,128,128]{2,1,0:T(8,128)(2,1)S(1)} custom-call(s32[1]{0:T(128)} %bitcast.5.core_ref, bf16[2,1536,128]{2,1,0:T(8,128)(2,1)S(1)} %bitcast.10, bf16[512,128]{1,0:T(8,128)(2,1)S(1)} %get-tuple-element.16.lhs_ref, bf16[1536,128]{1,0:T(8,128)(2,1)S(1)} %get-tuple-element.15.share_ref, bf16[128,1024]{1,0:T(8,128)(2,1)S(1)} %get-tuple-element.17.mixer_ref, ...), custom_call_target="tpu_custom_call" | custom-call | tf_op jit(solution)/shard_map/pallas_call | solution.py:168
  38.8 11.2 %all_to_all.11 = bf16[8,4,64,128]{3,2,1,0:T(8,128)(2,1)S(1)} all-to-all(bf16[8,4,64,128]{3,2,1,0:T(8,128)(2,1)S(1)} %bitcast.11), channel_id=1, replica_groups={{0,2,4,6,64,66,68,70},{1,3,5,7,65,67,69,71},{8,10,12,14,72,74,76,78},{9..., dimensions={0} | all-to-all | bytes 1048576 | tf_op jit(solution)/shard_map/all_to_all | solution.py:180
  50.1 0.8 %copy.7 = bf16[4,8,64,128]{3,2,1,0:T(8,128)(2,1)} copy(bf16[4,8,64,128]{3,2,0,1:T(8,128)(2,1)S(1)} %bitcast.12) | data formatting | bytes 1048576 | tf_op jit(solution)/shard_map/transpose | solution.py:181
Async XLA Ops:
  1.6 30.1 %copy-start = (bf16[1024,128]{1,0:T(8,128)(2,1)S(1)}, bf16[1024,128]{1,0:T(8,128)(2,1)}, u32[]{:S(2)}) copy-start(bf16[1024,128]{1,0:T(8,128)(2,1)} %mix_ref.1) | copy-start | bytes 786436

commit v8 on v7

--- a/solution.py
+++ b/solution.py
@@ -7,7 +7,7 @@
 
 Y, Z, X, C = 2, 8, 4, 2
 F32, BF16 = jnp.float32, jnp.bfloat16
-ORDER = [(y, z, x) for y in reversed(range(Y)) for z in reversed(range(Z)) for x in range(X)]
+ORDER = [(y, z, x) for z in reversed(range(Z)) for y in reversed(range(Y)) for x in range(X)]
 PLACE = [[[ORDER.index((y, z, x)) for x in range(X)] for z in range(Z)] for y in range(Y)]
 CHIP = [[((y * Z + z) * X + x) * C + c for y, z, x in ORDER] for c in range(C)]
 COLUMN = [[((y * Z + z) * X + x) * C + c for y in range(Y) for x in range(X)] for z in range(Z) for c in range(C)]

time: 51.8 us -> 51.3 us (level)
    all_to_all x1, blocking collectives: 30.1 us -> 29.4 us  [body(): lax.all_to_all(message, 'res', split_axis=0, concat_axis=0, tiled=True, a...]
where the time goes in v8:
time: 51.3 us; the launch traced here: 50.4 us
  blocking collectives  44.6 us (87%)
  Pallas kernels  4.97 us (10%)
  local copies, waits for them, and re-layouts  0.84 us (2%)
    all_to_all x1, blocking collectives, body(): lax.all_to_all(message, 'res', split_axis=0, concat_axis=0, tiled=True, a...  29.4 us
    all_to_all x1, blocking collectives, body(): lax.all_to_all(tile, 'res', split_axis=0, concat_axis=0, tiled=True, axis...  11.5 us
    all_gather x1, blocking collectives, body(): lax.all_gather(share, 'res', axis=0, tiled=False, axis_index_groups=PAIR)  3.66 us
    pallas_call x1, Pallas kernels, body(): pl.pallas_call(pair_kernel, out_shape=jax.ShapeDtypeStruct((16, 128, 128)...  2.02 us
    pallas_call x1, Pallas kernels, body(): pl.pallas_call(project_kernel, out_shape=(jax.ShapeDtypeStruct((64, 32, 1...  1.6 us
    pallas_call x1, Pallas kernels, body(): pl.pallas_call(share_kernel, out_shape=(jax.ShapeDtypeStruct((512, 128),...  1.34 us

profile of v8, /device:TPU:1, one launch (start us, length us, event | category | flops | bytes accessed | tf_op | source)
XLA Modules:
  0.0 50.4 jit_solution(2510408593765195629)
XLA Ops:
  0.0 1.6 %shard_map.64 = (bf16[64,32,128]{2,1,0:T(8,128)(2,1)S(1)}, f32[1,128]{1,0:T(1,128)S(1)}) custom-call(bf16[512,256]{1,0:T(8,128)(2,1)} %bitcast.13, f32[1,256]{1,0:T(1,128)} %bitcast.16, bf16[32,256]{1,0:T(8,128)(2,1)} %bitcast.14, bf16[32,256]{1,0:T(8,128)(2,1)} %bitcast.15, f32[1,128]{1,0:T(1,128)} %bitcast.17), custom_call_target="tpu_custom_call" | custom-call | tf_op jit(solution)/shard_map/pallas_call | solution.py:129
  1.6 0.0 copy-start
  1.6 29.4 %all_to_all.10.own_ref = bf16[64,32,128]{2,1,0:T(8,128)(2,1)S(1)} all-to-all(bf16[64,32,128]{2,1,0:T(8,128)(2,1)S(1)} %get-tuple-element.14), channel_id=1, replica_groups={{120,122,124,126,56,58,60,62,112,114,116,118,48,50,52,54,104,106,108,11..., dimensions={0} | all-to-all | bytes 1048576 | tf_op jit(solution)/shard_map/all_to_all | solution.py:154
  31.0 0.0 copy-done
  31.0 1.3 %shard_map.65 = (bf16[512,128]{1,0:T(8,128)(2,1)S(1)}, bf16[1536,128]{1,0:T(8,128)(2,1)S(1)}, bf16[128,1024]{1,0:T(8,128)(2,1)S(1)}) custom-call(s32[1]{0:T(128)} %bitcast.5.core_ref, bf16[64,32,128]{2,1,0:T(8,128)(2,1)S(1)} %all_to_all.10.own_ref, bf16[1024,128]{1,0:T(8,128)(2,1)S(1)} %copy-done), custom_call_target="tpu_custom_call" | custom-call | tf_op jit(solution)/shard_map/pallas_call | solution.py:155
  32.3 3.7 %all-gather = bf16[3072,128]{1,0:T(8,128)(2,1)S(1)} all-gather(bf16[1536,128]{1,0:T(8,128)(2,1)S(1)} %get-tuple-element.15.share_ref), channel_id=2, replica_groups={{0,1},{2,3},{4,5},{6,7},{8,9},{10,11},{12,13},{14,15},{16,17},{18,19},{..., dimensions={0}, use_global_device_ids=true | all-gather | bytes 1179648 | tf_op jit(solution)/shard_map/all_gather | solution.py:167
  36.0 2.0 %shard_map.66 = bf16[16,128,128]{2,1,0:T(8,128)(2,1)S(1)} custom-call(s32[1]{0:T(128)} %bitcast.5.core_ref, bf16[2,1536,128]{2,1,0:T(8,128)(2,1)S(1)} %bitcast.10, bf16[512,128]{1,0:T(8,128)(2,1)S(1)} %get-tuple-element.16.lhs_ref, bf16[1536,128]{1,0:T(8,128)(2,1)S(1)} %get-tuple-element.15.share_ref, bf16[128,1024]{1,0:T(8,128)(2,1)S(1)} %get-tuple-element.17.mixer_ref, ...), custom_call_target="tpu_custom_call" | custom-call | tf_op jit(solution)/shard_map/pallas_call | solution.py:168
  38.0 11.5 %all_to_all.11 = bf16[8,4,64,128]{3,2,1,0:T(8,128)(2,1)S(1)} all-to-all(bf16[8,4,64,128]{3,2,1,0:T(8,128)(2,1)S(1)} %bitcast.11), channel_id=1, replica_groups={{0,2,4,6,64,66,68,70},{1,3,5,7,65,67,69,71},{8,10,12,14,72,74,76,78},{9..., dimensions={0} | all-to-all | bytes 1048576 | tf_op jit(solution)/shard_map/all_to_all | solution.py:180
  49.6 0.8 %copy.7 = bf16[4,8,64,128]{3,2,1,0:T(8,128)(2,1)} copy(bf16[4,8,64,128]{3,2,0,1:T(8,128)(2,1)S(1)} %bitcast.12) | data formatting | bytes 1048576 | tf_op jit(solution)/shard_map/transpose | solution.py:181
Async XLA Ops:
  1.6 29.4 %copy-start = (bf16[1024,128]{1,0:T(8,128)(2,1)S(1)}, bf16[1024,128]{1,0:T(8,128)(2,1)}, u32[]{:S(2)}) copy-start(bf16[1024,128]{1,0:T(8,128)(2,1)} %mix_ref.1) | copy-start | bytes 786436
